TPU v7x, 128 devices: a whole 4x4x4 slice. The times are simulated.
128 devices in a mesh: lat: 8 (over z_lo, x), lon: 16 (over z_hi, y, core).
Axes of the slice: x: 4, y: 4, z: 4 (z_hi: 2, z_lo: 2; z = z_hi * 2 + z_lo), core: 2. Of those that a mesh axis runs over, the one named last changes fastest.
Arguments:
- fields: float32 [384, 768, 128], P('lat', 'lon'), may hold values from -6 to 6
- diffusion: float32 [128], replicated, may hold values from 0.3 to 30
- wave_slots: int32 [256], replicated, may hold values from 0 to 255, as said below
- reservoir_state: bfloat16 [192, 384, 4096], P('lat', 'lon'), may hold values from -0.8984375 to 0.8984375
- adjacency_blocks: bfloat16 [32, 8, 128, 128], replicated, may hold values from -0.1875 to 0.1875
- adjacency_index: int32 [32, 8], replicated, may hold values from 0 to 31, as said below
- input_index: int32 [4096], replicated, may hold values from 0 to 4607
- input_gain: float32 [4096], replicated, may hold values from -1.5 to 1.5
- bias: float32 [4096], replicated, may hold values from -0.5 to 0.5
- readout: bfloat16 [4096, 512], replicated, may hold values from -0.09375 to 0.09375
Outputs:
- blended_prediction: float32 [384, 768, 128], P('lat', 'lon')
- reservoir_next: bfloat16 [192, 384, 4096], P('lat', 'lon')
- spectral: float32 [256, 2, 256, 128], P(('lat', 'lon'))
Inputs may be any that keep to these rules, and one draw needn't show every extreme that they name: `wave_slots`: a permutation of the wavenumbers in which slots 2 k and 2 k + 1 hold wavenumbers adding up to 255. `adjacency_index`: row g names block g and 7 other blocks, all different.
All inputs are finite; a program needn't handle non-finite values.
Results may differ from a plain program's by a relative error of at most 0.004.
The roundings to bfloat16 on the way count: a program that leaves them out, or rounds other values in their place, can miss the bound.
Values may be sent and summed in bfloat16 or wider, within the bound.
A program may use at most 256 MiB of HBM per device.

v0:
```python
import functools
import math

import jax
import jax.numpy as jnp
import numpy as np
from jax import lax
from jax.experimental import pallas as pl
from jax.experimental.pallas import tpu as pltpu
from jax.sharding import PartitionSpec as P

ROWS = 384
COLS = 768
WAVES = 256
CHANNELS = 128
RES = 4096
BLOCK = 128
CONN = 8
TILE = 2
WINDOW = 6
LATS = 8
LONS = 16
DEVICES = LATS * LONS
SUB_ROWS = ROWS // DEVICES
BAND = 48
HALF = 28
SENT_COLS = 2 * HALF
TILES = 24
FRAME = TILES + 2
CHUNK = 512
CHUNKS = RES // CHUNK
PICK = 2 * WINDOW * CHANNELS
MB = 1 << 20


def geometry():
    j = np.arange(ROWS).reshape(DEVICES, SUB_ROWS).T.reshape(-1)
    colatitude = (j + 0.5) * (math.pi / ROWS)
    return np.cos(colatitude), np.sin(colatitude)


def order_rows():
    m = np.arange(WAVES)[:, None].astype(np.float64)
    n = np.arange(WAVES)[None, :].astype(np.float64)
    above = n > m
    above_sq = np.where(above, 4 * n * n - 1, 0.0)
    a = np.sqrt(above_sq / np.where(above, n * n - m * m, 1.0))
    b = np.sqrt(
        np.where(above, (n - 1) ** 2 - m * m, 0.0) / np.where(n > 1.5, 4 * (n - 1) ** 2 - 1, 1.0)
    )
    e = (n == m).astype(np.float64)
    factors = np.concatenate([a, a * b, e], axis=1)
    _, sin_col = geometry()
    halves = np.arange(1, WAVES)
    logs = np.concatenate([[0.0], np.cumsum(np.log1p(0.5 / halves))])
    pole = np.exp(0.5 * logs[:, None] + m * np.log(sin_col)[None, :] - 0.5 * math.log(2.0))
    return factors.astype(np.float32), pole.astype(np.float32)


def forward_rows():
    m = np.arange(WAVES)[:, None]
    k = np.arange(COLS)[None, :]
    angle = (m * k % COLS) * (2.0 * math.pi / COLS)
    table = np.stack([np.cos(angle), -np.sin(angle)], axis=1) / COLS
    return table.reshape(2 * WAVES, COLS)


def inverse_columns():
    o = np.arange(LONS)[:, None, None]
    b = np.arange(2)[None, :, None]
    t = np.arange(HALF)[None, None, :]
    k = ((BAND * o - 2 + 2 * t + b) % COLS).reshape(-1)
    m = np.arange(WAVES)[None, :]
    angle = (m * k[:, None] % COLS) * (2.0 * math.pi / COLS)
    factor = np.where(m == 0, 1.0, 2.0)
    table = np.stack([factor * np.cos(angle), -factor * np.sin(angle)], axis=2)
    return table.reshape(LONS * SENT_COLS, 2 * WAVES)


def legendre_kernel(factor_ref, pole_ref, cos_ref, weight_ref, table_ref, weighted_ref, rows_ref):
    cos_col = cos_ref[...]
    poles = [pole_ref[pl.ds(s, 1), :] for s in range(2)]

    def eight(base, carry):
        state = list(carry)
        stacked = [[], []]
        for step in range(8):
            n = base * 8 + step
            for s in range(2):
                previous, current = state[s]
                a = factor_ref[s, n]
                ab = factor_ref[s, WAVES + n]
                e = factor_ref[s, 2 * WAVES + n]
                value = a * (cos_col * current) - ab * previous + e * poles[s]
                state[s] = (current, value)
                stacked[s].append(value)
        for s in range(2):
            rows_ref[s, pl.ds(pl.multiple_of(base * 8, 8), 8), :] = jnp.concatenate(
                stacked[s], axis=0
            )
        return tuple(state)

    zero = jnp.zeros((1, ROWS), jnp.float32)
    lax.fori_loop(0, WAVES // 8, eight, ((zero, zero), (zero, zero)))
    for s in range(2):
        rows = rows_ref[s]
        table_ref[s] = rows.astype(jnp.bfloat16)
        weighted_ref[s] = (rows * weight_ref[...]).astype(jnp.bfloat16)


def dft_kernel(table_ref, rows_ref, out_ref):
    data = rows_ref[...]
    whole = jnp.concatenate(
        [data[:, r].reshape(COLS, CHANNELS) for r in range(SUB_ROWS)], axis=1
    )
    out_ref[...] = jnp.dot(
        table_ref[...], whole, preferred_element_type=jnp.float32
    ).astype(jnp.bfloat16)


def spectral_kernel(
    owned_ref, weighted_ref, table_ref, diffusion_ref, spectral_ref, grid_ref, wide_ref, back_ref
):
    for r in range(SUB_ROWS):
        wide_ref[r] = owned_ref[:, r * 128 : (r + 1) * 128].astype(jnp.float32)
    degree = lax.broadcasted_iota(jnp.int32, (WAVES, CHANNELS), 0).astype(jnp.float32)
    scaled = degree * (degree + 1.0) / float((WAVES - 1) * WAVES)
    damping = 1.0 / (1.0 + diffusion_ref[...] * (scaled * scaled))
    damping = jnp.concatenate([damping, damping], axis=1)
    for s in range(2):
        parts = []
        for p in range(2):
            parts.append(
                jnp.concatenate(
                    [
                        wide_ref[r, pl.ds(2 * s + p, DEVICES, stride=4), :]
                        for r in range(SUB_ROWS)
                    ],
                    axis=0,
                )
            )
        zonal = jnp.concatenate(parts, axis=1).astype(jnp.bfloat16)
        filtered = damping * jnp.dot(
            weighted_ref[s], zonal, preferred_element_type=jnp.float32
        )
        for p in range(2):
            spectral_ref[s, p] = filtered[:, p * 128 : (p + 1) * 128]
        grid = lax.dot_general(
            table_ref[s],
            filtered.astype(jnp.bfloat16),
            (((0,), (0,)), ((), ())),
            preferred_element_type=jnp.float32,
        )
        for p in range(2):
            for r in range(SUB_ROWS):
                back_ref[r, pl.ds(2 * s + p, DEVICES, stride=4), :] = grid[
                    r * 128 : (r + 1) * 128, p * 128 : (p + 1) * 128
                ]
    for r in range(SUB_ROWS):
        grid_ref[:, r * 128 : (r + 1) * 128] = back_ref[r].astype(jnp.bfloat16)


def recur_kernel(index_ref, state_ref, blocks_ref, key_ref, recur_ref, pick_ref):
    chunk = pl.program_id(0)
    per = CHUNK // BLOCK
    for g in range(per):
        columns = []
        for l in range(CONN):
            at = index_ref[chunk * per + g, l]
            columns.append(state_ref[:, pl.ds(pl.multiple_of(at * BLOCK, BLOCK), BLOCK)])
        left = jnp.concatenate(columns, axis=1)
        right = jnp.concatenate([blocks_ref[g, l] for l in range(CONN)], axis=1)
        recur_ref[:, g * BLOCK : (g + 1) * BLOCK] = lax.dot_general(
            left, right, (((1,), (1,)), ((), ())), preferred_element_type=jnp.float32
        )
    entry = lax.broadcasted_iota(jnp.int32, (PICK, CHUNK), 0)
    pick_ref[...] = jnp.where(entry == key_ref[...], 1.0, 0.0).astype(jnp.bfloat16)


def reservoir_kernel(
    rows_ref,
    low_ref,
    high_ref,
    pick_ref,
    recur_ref,
    node_ref,
    gain_ref,
    readout_ref,
    blend_ref,
    next_ref,
    frame_ref,
    drive_ref,
    total_ref,
):
    chunk = pl.program_id(0)

    @pl.when(chunk == 0)
    def _():
        def row_of(position):
            if position < 2:
                part = low_ref[:, position * 128 : (position + 1) * 128]
            elif position >= BAND + 2:
                at = position - BAND - 2
                part = high_ref[:, at * 128 : (at + 1) * 128]
            else:
                j = position - 2
                at = j % SUB_ROWS
                part = rows_ref[j // SUB_ROWS, :, at * 128 : (at + 1) * 128]
            return part.astype(jnp.float32)

        for pair in range(FRAME // 2):
            for a in range(2):
                upper = row_of(4 * pair + a)
                lower = row_of(4 * pair + 2 + a)
                for b in range(WINDOW):
                    start = (b % 2) * HALF + b // 2
                    both = jnp.concatenate(
                        [upper[start : start + TILES], lower[start : start + TILES]], axis=0
                    )
                    at = (b * 2 + a) * 128
                    frame_ref[pair * 48 : (pair + 1) * 48, at : at + 128] = both.astype(
                        jnp.bfloat16
                    )
        total_ref[...] = jnp.zeros_like(total_ref)

    drive_ref[...] = jnp.dot(frame_ref[...], pick_ref[...], preferred_element_type=jnp.float32)
    count = TILES * TILES
    row = node_ref[...]
    picked = jnp.where(
        row == 0,
        drive_ref[0:count],
        jnp.where(row == 1, drive_ref[TILES : count + TILES], drive_ref[2 * TILES :]),
    )
    upcoming = jnp.tanh(recur_ref[...] + picked * gain_ref[0:1, :] + gain_ref[1:2, :]).astype(
        jnp.bfloat16
    )
    next_ref[...] = upcoming
    total_ref[...] += jnp.dot(upcoming, readout_ref[...], preferred_element_type=jnp.float32)

    @pl.when(chunk == CHUNKS - 1)
    def _():
        for a in range(2):
            for b in range(2):
                at = ((2 + b) * 2 + a) * 128
                forecast = frame_ref[:, at : at + 128].astype(jnp.float32)
                to = (a * 2 + b) * 128
                for i in range(TILES):
                    blend_ref[pl.ds((2 * i + a) * BAND + b, TILES, stride=2), :] = (
                        forecast[(i + 1) * TILES : (i + 2) * TILES]
                        + total_ref[i * TILES : (i + 1) * TILES, to : to + 128]
                    )


def shards(
    fields,
    diffusion,
    wave_slots,
    reservoir_state,
    adjacency_blocks,
    adjacency_index,
    input_index,
    input_gain,
    bias,
    readout,
):
    vmem = pl.BlockSpec(memory_space=pltpu.VMEM)
    smem = pl.BlockSpec(memory_space=pltpu.SMEM)
    lat = lax.axis_index("lat")
    owner = lat * LONS + lax.axis_index("lon")

    sent = fields.reshape(LONS, SUB_ROWS * BAND, CHANNELS).astype(jnp.bfloat16)
    row_data = lax.all_to_all(sent, "lon", split_axis=0, concat_axis=0, tiled=True)

    slot_part = (2 * wave_slots[:, None] + jnp.arange(2, dtype=jnp.int32)).reshape(-1)
    chosen = (
        slot_part[:, None] == jnp.arange(2 * WAVES, dtype=jnp.int32)[None, :]
    ).astype(jnp.bfloat16)
    forward = jnp.dot(chosen, jnp.asarray(forward_rows(), jnp.bfloat16)).astype(jnp.bfloat16)
    inverse = lax.dot_general(
        jnp.asarray(inverse_columns(), jnp.bfloat16), chosen, (((1,), (1,)), ((), ()))
    ).astype(jnp.bfloat16)
    factors, poles = order_rows()
    factors, poles = jnp.asarray(factors), jnp.asarray(poles)
    owned = lax.dynamic_slice_in_dim(wave_slots, owner * 2, 2)
    own_factors = jnp.concatenate(
        [lax.dynamic_slice_in_dim(factors, owned[s], 1) for s in range(2)], axis=0
    )
    own_poles = jnp.concatenate(
        [lax.dynamic_slice_in_dim(poles, owned[s], 1) for s in range(2)], axis=0
    )
    cos_col, sin_col = geometry()
    table_shape = jax.ShapeDtypeStruct((2, WAVES, ROWS), jnp.bfloat16)
    table, weighted = pl.pallas_call(
        legendre_kernel,
        out_shape=(table_shape, table_shape),
        in_specs=[smem, vmem, vmem, vmem],
        out_specs=(vmem, vmem),
        scratch_shapes=[pltpu.VMEM((2, WAVES, ROWS), jnp.float32)],
        cost_estimate=pl.CostEstimate(flops=2000000, bytes_accessed=800000, transcendentals=0),
        name="legendre",
    )(
        own_factors,
        own_poles,
        jnp.asarray(cos_col[None, :], jnp.float32),
        jnp.asarray((math.pi / ROWS) * sin_col[None, :], jnp.float32),
    )

    states = reservoir_state.reshape(TILES * TILES, RES)
    row_at = input_index // (WINDOW * CHANNELS)
    col_at = input_index // CHANNELS % WINDOW
    key = (col_at * 2 + row_at % 2) * CHANNELS + input_index % CHANNELS
    recur, pick = pl.pallas_call(
        recur_kernel,
        grid=(CHUNKS,),
        out_shape=(
            jax.ShapeDtypeStruct((TILES * TILES, RES), jnp.float32),
            jax.ShapeDtypeStruct((PICK, RES), jnp.bfloat16),
        ),
        in_specs=[
            smem,
            pl.BlockSpec((TILES * TILES, RES), lambda c: (0, 0)),
            pl.BlockSpec((CHUNK // BLOCK, CONN, BLOCK, BLOCK), lambda c: (c, 0, 0, 0)),
            pl.BlockSpec((1, CHUNK), lambda c: (0, c)),
        ],
        out_specs=(
            pl.BlockSpec((TILES * TILES, CHUNK), lambda c: (0, c)),
            pl.BlockSpec((PICK, CHUNK), lambda c: (0, c)),
        ),
        compiler_params=pltpu.CompilerParams(vmem_limit_bytes=32 * MB),
        cost_estimate=pl.CostEstimate(
            flops=2 * TILES * TILES * RES * CONN * BLOCK,
            bytes_accessed=36 * MB,
            transcendentals=0,
        ),
        name="recur",
    )(adjacency_index, states, adjacency_blocks, key[None, :])

    zonal = pl.pallas_call(
        dft_kernel,
        out_shape=jax.ShapeDtypeStruct((2 * WAVES, SUB_ROWS * CHANNELS), jnp.bfloat16),
        in_specs=[vmem, vmem],
        out_specs=vmem,
        name="dft",
    )(forward, row_data.reshape(LONS, SUB_ROWS, BAND, CHANNELS))
    owned_coef = lax.all_to_all(
        zonal.reshape(DEVICES, 4, SUB_ROWS * CHANNELS),
        ("lat", "lon"),
        split_axis=0,
        concat_axis=0,
        tiled=True,
    )
    spectral, grid_part = pl.pallas_call(
        spectral_kernel,
        out_shape=(
            jax.ShapeDtypeStruct((2, 2, WAVES, CHANNELS), jnp.float32),
            jax.ShapeDtypeStruct((4 * DEVICES, SUB_ROWS * CHANNELS), jnp.bfloat16),
        ),
        in_specs=[vmem, vmem, vmem, vmem],
        out_specs=(vmem, vmem),
        scratch_shapes=[
            pltpu.VMEM((SUB_ROWS, 4 * DEVICES, CHANNELS), jnp.float32),
            pltpu.VMEM((SUB_ROWS, 4 * DEVICES, CHANNELS), jnp.float32),
        ],
        name="spectral",
    )(
        owned_coef.reshape(4 * DEVICES, SUB_ROWS * CHANNELS),
        weighted,
        table,
        diffusion[None, :],
    )
    back = lax.all_to_all(
        grid_part.reshape(DEVICES, 4, SUB_ROWS * CHANNELS),
        ("lat", "lon"),
        split_axis=0,
        concat_axis=0,
        tiled=True,
    )
    samples = jnp.dot(
        inverse,
        back.reshape(4 * DEVICES, SUB_ROWS * CHANNELS),
        preferred_element_type=jnp.float32,
    ).astype(jnp.bfloat16)
    framed = lax.all_to_all(
        samples.reshape(LONS, SENT_COLS, SUB_ROWS * CHANNELS),
        "lon",
        split_axis=0,
        concat_axis=0,
        tiled=True,
    )
    up = [(i, i + 1) for i in range(LATS - 1)]
    down = [(i + 1, i) for i in range(LATS - 1)]
    low = lax.ppermute(framed[LONS - 1, :, CHANNELS:], "lat", up)
    high = lax.ppermute(framed[0, :, : 2 * CHANNELS], "lat", down)

    const = lambda *zeros: (lambda c: zeros)
    blended, upcoming = pl.pallas_call(
        reservoir_kernel,
        grid=(CHUNKS,),
        out_shape=(
            jax.ShapeDtypeStruct((BAND * BAND, CHANNELS), jnp.float32),
            jax.ShapeDtypeStruct((TILES * TILES, RES), jnp.bfloat16),
        ),
        in_specs=[
            pl.BlockSpec((LONS, SENT_COLS, SUB_ROWS * CHANNELS), const(0, 0, 0)),
            pl.BlockSpec((SENT_COLS, 2 * CHANNELS), const(0, 0)),
            pl.BlockSpec((SENT_COLS, 2 * CHANNELS), const(0, 0)),
            pl.BlockSpec((PICK, CHUNK), lambda c: (0, c)),
            pl.BlockSpec((TILES * TILES, CHUNK), lambda c: (0, c)),
            pl.BlockSpec((1, CHUNK), lambda c: (0, c)),
            pl.BlockSpec((2, CHUNK), lambda c: (0, c)),
            pl.BlockSpec((CHUNK, 4 * CHANNELS), lambda c: (c, 0)),
        ],
        out_specs=(
            pl.BlockSpec((BAND * BAND, CHANNELS), const(0, 0)),
            pl.BlockSpec((TILES * TILES, CHUNK), lambda c: (0, c)),
        ),
        scratch_shapes=[
            pltpu.VMEM((FRAME * TILES, PICK), jnp.bfloat16),
            pltpu.VMEM((FRAME * TILES, CHUNK), jnp.float32),
            pltpu.VMEM((TILES * TILES, 4 * CHANNELS), jnp.float32),
        ],
        compiler_params=pltpu.CompilerParams(vmem_limit_bytes=32 * MB),
        cost_estimate=pl.CostEstimate(
            flops=2 * FRAME * TILES * RES * PICK,
            bytes_accessed=36 * MB,
            transcendentals=TILES * TILES * RES,
        ),
        name="reservoir",
    )(
        framed,
        low,
        high,
        pick,
        recur,
        (row_at // 2)[None, :],
        jnp.stack([input_gain, bias]),
        readout,
    )
    return (
        blended.reshape(BAND, BAND, CHANNELS),
        upcoming.reshape(TILES, TILES, RES),
        spectral,
    )


def solution(mesh):
    placed = (P("lat", "lon", None), P(), P(), P("lat", "lon", None), P(), P(), P(), P(), P(), P())
    return jax.shard_map(
        shards,
        mesh=mesh,
        in_specs=placed,
        out_specs=(
            P("lat", "lon", None),
            P("lat", "lon", None),
            P(("lat", "lon"), None, None, None),
        ),
        check_vma=False,
    )
```

profile of v0, /device:TPU:40, one launch (start us, length us, event | category | flops | bytes accessed | tf_op | source)
XLA Modules:
  0.0 137.8 jit_solution(1231809136019177446)
XLA Ops:
  0.6 2.2 %convert_element_type.10 = bf16[48,48,128]{2,1,0:T(8,128)(2,1)} convert(f32[48,48,128]{2,1,0:T(8,128)} %param.16) | non-fusion elementwise | flops 294912 | bytes 1769472 | tf_op jit(solution)/shard_map/convert_element_type | solution.py:271
  2.8 7.3 %all-to-all-start = ((bf16[16,144,128]{2,1,0:T(8,128)(2,1)}), bf16[16,144,128]{2,1,0:T(8,128)(2,1)S(1)}, u32[]{:S(2)}, u32[]{:S(2)}) async-start(bf16[16,144,128]{2,1,0:T(8,128)(2,1)} %bitcast), calls=%async_computation | async-start | bytes 1179648 | tf_op jit(solution)/shard_map/all_to_all | solution.py:272
  16.3 2.7 %fusion.2.table_ref = bf16[512,768]{1,0:T(8,128)(2,1)} fusion(bf16[512,768]{1,0:T(8,128)(2,1)} %constant.89.clone, s32[512]{0:T(512)S(1)} %add.60), kind=kOutput, calls=%fused_computation.3 | convolution fusion | flops 402915328 | bytes 1574912 | tf_op jit(solution)/shard_map/dot_general | solution.py:278
  20.2 2.6 %dft.1 = bf16[512,384]{1,0:T(8,128)(2,1)} custom-call(bf16[512,768]{1,0:T(8,128)(2,1)} %fusion.2.table_ref, bf16[16,3,48,128]{3,2,1,0:T(8,128)(2,1)} %bitcast.23), custom_call_target="tpu_custom_call" | custom-call | tf_op jit(solution)/shard_map/dft/pallas_call | solution.py:338
  22.8 1.8 %reshape.52 = bf16[128,4,384]{2,1,0:T(4,128)(2,1)} reshape(bf16[512,384]{1,0:T(8,128)(2,1)} %dft.1) | data formatting | bytes 786432 | tf_op jit(solution)/shard_map/reshape | solution.py:346
  24.6 9.8 %all-to-all-start.1 = ((bf16[128,4,384]{2,1,0:T(4,128)(2,1)}), bf16[128,4,384]{2,1,0:T(4,128)(2,1)S(1)}, u32[]{:S(2)}, u32[]{:S(2)}) async-start(bf16[128,4,384]{2,1,0:T(4,128)(2,1)} %reshape.52), calls=%async_computation.1 | async-start | bytes 786432 | tf_op jit(solution)/shard_map/all_to_all | solution.py:345
  37.1 4.7 %legendre.1 = (bf16[2,256,384]{2,1,0:T(8,128)(2,1)}, bf16[2,256,384]{2,1,0:T(8,128)(2,1)}) custom-call(f32[2,768]{1,0:T(2,128)} %pad_maximum_fusion.1.factor_ref, f32[2,384]{1,0:T(2,128)} %pad_maximum_fusion.2.pole_ref, f32[1,384]{1,0:T(1,128)} %constant.93.clone.cos_ref, f32[1,384]{1,0:T(1,128)} %constant.94.clone.weight_ref), custom_call_target="tpu_custom_call" | custom-call | flops 2000000 | bytes 800000 | tf_op jit(solution)/shard_map/legendre/pallas_call | solution.py:293
  41.8 2.7 %all-to-all-done.1 = bf16[128,4,384]{2,1,0:T(4,128)(2,1)S(1)} async-done(((bf16[128,4,384]{2,1,0:T(4,128)(2,1)}), bf16[128,4,384]{2,1,0:T(4,128)(2,1)S(1)}, u32[]{:S(2)}, u32[]{:S(2)}) %all-to-all-start.1) | async-done | bytes 393248 | tf_op jit(solution)/shard_map/all_to_all | solution.py:345
  45.3 2.9 %spectral.1 = (f32[2,2,256,128]{3,2,1,0:T(8,128)}, bf16[512,384]{1,0:T(8,128)(2,1)}) custom-call(bf16[512,384]{1,0:T(8,128)(2,1)} %reshape.53.owned_ref, bf16[2,256,384]{2,1,0:T(8,128)(2,1)} %get-tuple-element.11.weighted_ref, bf16[2,256,384]{2,1,0:T(8,128)(2,1)} %get-tuple-element.12.table_ref, f32[1,128]{1,0:T(1,128)} %bitcast.26), custom_call_target="tpu_custom_call" | custom-call | tf_op jit(solution)/shard_map/spectral/pallas_call | solution.py:352
  48.3 1.8 %reshape.54 = bf16[128,4,384]{2,1,0:T(4,128)(2,1)} reshape(bf16[512,384]{1,0:T(8,128)(2,1)} %get-tuple-element.13) | data formatting | bytes 786432 | tf_op jit(solution)/shard_map/reshape | solution.py:372
  50.1 7.1 %all-to-all-start.2 = ((bf16[128,4,384]{2,1,0:T(4,128)(2,1)}), bf16[128,4,384]{2,1,0:T(4,128)(2,1)S(1)}, u32[]{:S(2)}, u32[]{:S(2)}) async-start(bf16[128,4,384]{2,1,0:T(4,128)(2,1)} %reshape.54), calls=%async_computation.2 | async-start | bytes 786432 | tf_op jit(solution)/shard_map/all_to_all | solution.py:371
  57.3 10.0 %all-to-all-done.2 = bf16[128,4,384]{2,1,0:T(4,128)(2,1)S(1)} async-done(((bf16[128,4,384]{2,1,0:T(4,128)(2,1)}), bf16[128,4,384]{2,1,0:T(4,128)(2,1)S(1)}, u32[]{:S(2)}, u32[]{:S(2)}) %all-to-all-start.2) | async-done | bytes 393248 | tf_op jit(solution)/shard_map/all_to_all | solution.py:371
  67.4 2.1 %convolution_convert_fusion = bf16[896,384]{1,0:T(8,128)(2,1)} fusion(bf16[512,384]{1,0:T(8,128)(2,1)S(1)} %reshape.55, bf16[896,512]{1,0:T(8,128)(2,1)S(1)} %copy-done.10, s32[512]{0:T(512)S(1)} %add.60), kind=kOutput, calls=%fused_computation | convolution fusion | flops 822689792 | bytes 2000896 | tf_op jit(solution)/shard_map/dot_general | solution.py:378
  69.5 5.0 %all-to-all-start.3 = ((bf16[16,56,384]{2,1,0:T(8,128)(2,1)}), bf16[16,56,384]{2,1,0:T(8,128)(2,1)S(1)}, u32[]{:S(2)}, u32[]{:S(2)}) async-start(bf16[16,56,384]{2,1,0:T(8,128)(2,1)} %bitcast.5), calls=%async_computation.3 | async-start | bytes 1376256 | tf_op jit(solution)/shard_map/all_to_all | solution.py:383
  74.6 3.4 %copy-done = bf16[32,8,128,128]{3,2,1,0:T(8,128)(2,1)S(1)} copy-done((bf16[32,8,128,128]{3,2,1,0:T(8,128)(2,1)S(1)}, bf16[32,8,128,128]{3,2,1,0:T(8,128)(2,1)}, u32[]{:S(2)}) %copy-start) | copy-done | bytes 8388632
  78.0 2.3 %copy-done.1 = bf16[24,24,4096]{2,1,0:T(8,128)(2,1)S(1)} copy-done((bf16[24,24,4096]{2,1,0:T(8,128)(2,1)S(1)}, bf16[24,24,4096]{2,1,0:T(8,128)(2,1)}, u32[]{:S(2)}) %copy-start.1) | copy-done | bytes 4718616
  80.3 19.4 %recur.1 = (f32[576,4096]{1,0:T(8,128)S(1)}, bf16[1536,4096]{1,0:T(8,128)(2,1)}) custom-call(s32[32,8]{1,0:T(8,128)S(1)} %copy.20.index_ref, bf16[576,4096]{1,0:T(8,128)(2,1)S(1)} %bitcast.22, bf16[32,8,128,128]{3,2,1,0:T(8,128)(2,1)S(1)} %copy-done, s32[1,4096]{1,0:T(1,128)S(1)} %bitcast.21), custom_call_target="tpu_custom_call" | custom-call | flops 4831838208 | bytes 37748736 | tf_op jit(solution)/shard_map/recur/pallas_call | solution.py:312
  99.7 3.6 %copy-done.3 = f32[576,4096]{1,0:T(8,128)} copy-done((f32[576,4096]{1,0:T(8,128)}, f32[576,4096]{1,0:T(8,128)S(1)}, u32[]{:S(2)}) %copy-start.3) | copy-done | bytes 9437208
  103.3 4.0 %collective-permute-start.1 = (bf16[56,256]{1,0:T(8,128)(2,1)S(1)}, bf16[56,256]{1,0:T(8,128)(2,1)S(1)}, u32[]{:S(2)}, u32[]{:S(2)}) collective-permute-start(bf16[56,256]{1,0:T(8,128)(2,1)S(1)} %get-tuple-element.21), channel_id=1, source_target_pairs={{16,0},{32,16},{48,32},{64,48},{80,64},{96,80},{112,96},{17,1},{33... | collective-permute-start | bytes 86024 | tf_op jit(solution)/shard_map/ppermute | solution.py:393
  107.3 1.9 %collective-permute-start = (bf16[56,256]{1,0:T(8,128)(2,1)S(1)}, bf16[56,256]{1,0:T(8,128)(2,1)S(1)}, u32[]{:S(2)}, u32[]{:S(2)}) collective-permute-start(bf16[56,256]{1,0:T(8,128)(2,1)S(1)} %get-tuple-element.22), channel_id=1, source_target_pairs={{0,16},{16,32},{32,48},{48,64},{64,80},{80,96},{96,112},{1,17},{17... | collective-permute-start | bytes 86024 | tf_op jit(solution)/shard_map/ppermute | solution.py:392
  109.3 5.9 %collective-permute-done.low_ref = bf16[56,256]{1,0:T(8,128)(2,1)S(1)} collective-permute-done((bf16[56,256]{1,0:T(8,128)(2,1)S(1)}, bf16[56,256]{1,0:T(8,128)(2,1)S(1)}, u32[]{:S(2)}, u32[]{:S(2)}) %collective-permute-start) | collective-permute-done | bytes 28704 | tf_op jit(solution)/shard_map/ppermute | solution.py:392
  115.2 2.2 %copy-done.2 = bf16[4096,512]{1,0:T(8,128)(2,1)S(1)} copy-done((bf16[4096,512]{1,0:T(8,128)(2,1)S(1)}, bf16[4096,512]{1,0:T(8,128)(2,1)}, u32[]{:S(2)}) %copy-start.2) | copy-done | bytes 4194328
  117.4 3.7 %copy-done.4 = f32[576,4096]{1,0:T(8,128)S(1)} copy-done((f32[576,4096]{1,0:T(8,128)S(1)}, f32[576,4096]{1,0:T(8,128)}, u32[]{:S(2)}) %copy-start.4) | copy-done | bytes 9437208
  121.1 16.7 %reservoir.1 = (f32[2304,128]{1,0:T(8,128)}, bf16[576,4096]{1,0:T(8,128)(2,1)}) custom-call(bf16[16,56,384]{2,1,0:T(8,128)(2,1)S(1)} %all-to-all-done.3.rows_ref, bf16[56,256]{1,0:T(8,128)(2,1)S(1)} %collective-permute-done.low_ref, bf16[56,256]{1,0:T(8,128)(2,1)S(1)} %collective-permute-done.1.high_ref, bf16[1536,4096]{1,0:T(8,128)(2,1)} %get-tuple-element.14.pick_ref, ...), custom_call_target="tpu_custom_call" | custom-call | flops 7851737088 | bytes 37748736 | tf_op jit(solution)/shard_map/reservoir/pallas_call | solution.py:396
  (35 shorter events, 7.2 us)
Async XLA Ops:
  2.8 16.6 %all-to-all-start = ((bf16[16,144,128]{2,1,0:T(8,128)(2,1)}), bf16[16,144,128]{2,1,0:T(8,128)(2,1)S(1)}, u32[]{:S(2)}, u32[]{:S(2)}) async-start(bf16[16,144,128]{2,1,0:T(8,128)(2,1)} %bitcast), calls=%async_computation | async-start | bytes 1179648 | tf_op jit(solution)/shard_map/all_to_all | solution.py:272
  14.7 42.4 %copy-start.9 = (s32[32,8]{0,1:T(8,128)S(1)}, s32[32,8]{0,1:T(8,128)}, u32[]{:S(2)}) copy-start(s32[32,8]{0,1:T(8,128)} %param.21) | copy-start | bytes 3076
  16.3 51.1 %copy-start.10 = (bf16[896,512]{1,0:T(8,128)(2,1)S(1)}, bf16[896,512]{1,0:T(8,128)(2,1)}, u32[]{:S(2)}) copy-start(bf16[896,512]{1,0:T(8,128)(2,1)} %constant.90.clone) | copy-start | bytes 2752516
  19.4 0.8 copy-start.5
  24.6 19.9 %all-to-all-start.1 = ((bf16[128,4,384]{2,1,0:T(4,128)(2,1)}), bf16[128,4,384]{2,1,0:T(4,128)(2,1)S(1)}, u32[]{:S(2)}, u32[]{:S(2)}) async-start(bf16[128,4,384]{2,1,0:T(4,128)(2,1)} %reshape.52), calls=%async_computation.1 | async-start | bytes 786432 | tf_op jit(solution)/shard_map/all_to_all | solution.py:345
  45.3 29.2 %copy-start.6 = (s32[4096]{0:T(1024)S(1)}, s32[4096]{0:T(1024)}, u32[]{:S(2)}) copy-start(s32[4096]{0:T(1024)} %param.22) | copy-start | bytes 49156
  50.1 17.2 %all-to-all-start.2 = ((bf16[128,4,384]{2,1,0:T(4,128)(2,1)}), bf16[128,4,384]{2,1,0:T(4,128)(2,1)S(1)}, u32[]{:S(2)}, u32[]{:S(2)}) async-start(bf16[128,4,384]{2,1,0:T(4,128)(2,1)} %reshape.54), calls=%async_computation.2 | async-start | bytes 786432 | tf_op jit(solution)/shard_map/all_to_all | solution.py:371
  69.5 33.8 %all-to-all-start.3 = ((bf16[16,56,384]{2,1,0:T(8,128)(2,1)}), bf16[16,56,384]{2,1,0:T(8,128)(2,1)S(1)}, u32[]{:S(2)}, u32[]{:S(2)}) async-start(bf16[16,56,384]{2,1,0:T(8,128)(2,1)} %bitcast.5), calls=%async_computation.3 | async-start | bytes 1376256 | tf_op jit(solution)/shard_map/all_to_all | solution.py:383
  74.6 3.4 %copy-start = (bf16[32,8,128,128]{3,2,1,0:T(8,128)(2,1)S(1)}, bf16[32,8,128,128]{3,2,1,0:T(8,128)(2,1)}, u32[]{:S(2)}) copy-start(bf16[32,8,128,128]{3,2,1,0:T(8,128)(2,1)} %blocks_ref.1) | copy-start | bytes 25165828
  78.0 2.3 %copy-start.1 = (bf16[24,24,4096]{2,1,0:T(8,128)(2,1)S(1)}, bf16[24,24,4096]{2,1,0:T(8,128)(2,1)}, u32[]{:S(2)}) copy-start(bf16[24,24,4096]{2,1,0:T(8,128)(2,1)} %param.19) | copy-start | bytes 14155780
  80.3 28.9 %copy-start.7 = (f32[4096]{0:T(1024)S(1)}, f32[4096]{0:T(1024)}, u32[]{:S(2)}) copy-start(f32[4096]{0:T(1024)} %param.24) | copy-start | bytes 49156
  80.3 28.9 %copy-start.8 = (f32[4096]{0:T(1024)S(1)}, f32[4096]{0:T(1024)}, u32[]{:S(2)}) copy-start(f32[4096]{0:T(1024)} %param.23) | copy-start | bytes 49156
  99.7 3.6 %copy-start.3 = (f32[576,4096]{1,0:T(8,128)}, f32[576,4096]{1,0:T(8,128)S(1)}, u32[]{:S(2)}) copy-start(f32[576,4096]{1,0:T(8,128)S(1)} %get-tuple-element.15.recur_ref) | copy-start | bytes 28311556
  103.3 6.0 %collective-permute-start.1 = (bf16[56,256]{1,0:T(8,128)(2,1)S(1)}, bf16[56,256]{1,0:T(8,128)(2,1)S(1)}, u32[]{:S(2)}, u32[]{:S(2)}) collective-permute-start(bf16[56,256]{1,0:T(8,128)(2,1)S(1)} %get-tuple-element.21), channel_id=1, source_target_pairs={{16,0},{32,16},{48,32},{64,48},{80,64},{96,80},{112,96},{17,1},{33... | collective-permute-start | bytes 86024 | tf_op jit(solution)/shard_map/ppermute | solution.py:393
  107.3 7.9 %collective-permute-start = (bf16[56,256]{1,0:T(8,128)(2,1)S(1)}, bf16[56,256]{1,0:T(8,128)(2,1)S(1)}, u32[]{:S(2)}, u32[]{:S(2)}) collective-permute-start(bf16[56,256]{1,0:T(8,128)(2,1)S(1)} %get-tuple-element.22), channel_id=1, source_target_pairs={{0,16},{16,32},{32,48},{48,64},{64,80},{80,96},{96,112},{1,17},{17... | collective-permute-start | bytes 86024 | tf_op jit(solution)/shard_map/ppermute | solution.py:392
  115.2 2.2 %copy-start.2 = (bf16[4096,512]{1,0:T(8,128)(2,1)S(1)}, bf16[4096,512]{1,0:T(8,128)(2,1)}, u32[]{:S(2)}) copy-start(bf16[4096,512]{1,0:T(8,128)(2,1)} %readout_ref.1) | copy-start | bytes 12582916
  117.4 3.7 %copy-start.4 = (f32[576,4096]{1,0:T(8,128)S(1)}, f32[576,4096]{1,0:T(8,128)}, u32[]{:S(2)}) copy-start(f32[576,4096]{1,0:T(8,128)} %copy-done.3) | copy-start | bytes 28311556
where the time goes:
time: 139 us; the launch traced here: 138 us
  Pallas kernels  46.4 us (33%)
  starting transfers between devices  35.1 us (25%)
  local copies, waits for them, and re-layouts  23.7 us (17%)
  waiting for transfers between devices  18.9 us (14%)
  matrix products  4.82 us (3%)
  between operations  4.68 us (3%)
  other arithmetic  4.23 us (3%)
    pallas_call x1, Pallas kernels, shards(): pl.pallas_call(recur_kernel, grid=(CHUNKS,), out_shape=(jax.ShapeDtypeStr...  19.4 us
    pallas_call x1, Pallas kernels, shards(): pl.pallas_call(reservoir_kernel, grid=(CHUNKS,), out_shape=(jax.ShapeDtyp...  16.7 us
    unnamed x23, local copies, waits for them, and re-layouts  16.1 us
    all_to_all x1, waiting for transfers between devices, shards(): lax.all_to_all(grid_part.reshape(DEVICES, 4, SUB_ROWS * CHANNELS), ('lat'...  10 us
    all_to_all x1, starting transfers between devices, shards(): lax.all_to_all(zonal.reshape(DEVICES, 4, SUB_ROWS * CHANNELS), ('lat', 'l...  9.76 us
    all_to_all x1, starting transfers between devices, shards(): lax.all_to_all(sent, 'lon', split_axis=0, concat_axis=0, tiled=True)  7.35 us
    all_to_all x1, starting transfers between devices, shards(): lax.all_to_all(grid_part.reshape(DEVICES, 4, SUB_ROWS * CHANNELS), ('lat'...  7.05 us
    ppermute x1, waiting for transfers between devices, shards(): low = lax.ppermute(framed[LONS - 1, :, CHANNELS:], 'lat', up)  5.87 us
  transfers between devices with their start and end apart: 6, of which 4 were waited for; matrix products, arithmetic and copies ran while one was open for 6% of the time, Pallas kernels for 17%

commit v1 on v0

v1 whole, which is shorter than its diff:
```python
import functools
import math

import jax
import jax.numpy as jnp
import numpy as np
from jax import lax
from jax.experimental import pallas as pl
from jax.experimental.pallas import tpu as pltpu
from jax.sharding import PartitionSpec as P

ROWS = 384
COLS = 768
WAVES = 256
CHANNELS = 128
RES = 4096
BLOCK = 128
CONN = 8
TILE = 2
WINDOW = 6
LATS = 8
LONS = 16
DEVICES = LATS * LONS
CHIPS = DEVICES // 2
SUB_ROWS = ROWS // DEVICES
BAND = 48
HALF = 28
SENT_COLS = 2 * HALF
TILES = 24
FRAME = TILES + 2
CHUNK = 512
CHUNKS = RES // CHUNK
PICK = 2 * WINDOW * CHANNELS
MB = 1 << 20
MESH = pl.DeviceIdType.MESH
SPLIT = (7, 16, 24, 32)
LANES = SUB_ROWS * CHANNELS
NODES = TILES * TILES


def geometry():
    j = np.arange(ROWS).reshape(CHIPS, 2, SUB_ROWS).transpose(2, 1, 0).reshape(-1)
    colatitude = (j + 0.5) * (math.pi / ROWS)
    return np.cos(colatitude), np.sin(colatitude)


def log_terms():
    index = np.arange(WAVES).astype(np.float64)
    return np.where(index > 0, np.log1p(0.5 / np.maximum(index, 1.0)), 0.0)


def forward_rows():
    m = np.arange(WAVES)[:, None]
    k = np.arange(COLS)[None, :]
    angle = (m * k % COLS) * (2.0 * math.pi / COLS)
    table = np.stack([np.cos(angle), -np.sin(angle)], axis=1) / COLS
    return table.reshape(2 * WAVES, COLS)


def inverse_columns():
    o = np.arange(LONS)[:, None, None]
    b = np.arange(2)[None, :, None]
    t = np.arange(HALF)[None, None, :]
    k = ((BAND * o - 2 + 2 * t + b) % COLS).reshape(-1)
    m = np.arange(WAVES)[None, :]
    angle = (m * k[:, None] % COLS) * (2.0 * math.pi / COLS)
    factor = np.where(m == 0, 1.0, 2.0)
    table = np.stack([factor * np.cos(angle), -factor * np.sin(angle)], axis=2)
    return table.reshape(LONS * SENT_COLS, 2 * WAVES)


def split(table):
    high = table.astype(jnp.bfloat16)
    return high, (table - high.astype(np.float32)).astype(jnp.bfloat16)


def chain_kernel(
    slots_ref,
    index_ref,
    fields_ref,
    column_ref,
    row_ref,
    forward_high_ref,
    forward_low_ref,
    inverse_ref,
    cos_ref,
    log_sin_ref,
    weight_ref,
    diffusion_ref,
    logs_ref,
    states_hbm,
    blocks_hbm,
    spectral_ref,
    framed_ref,
    halo_ref,
    recur_hbm,
    states_ref,
    blocks_ref,
    recur_ref,
    sent_ref,
    rows_ref,
    table_ref,
    factor_ref,
    legendre_ref,
    weighted_ref,
    plain_ref,
    zonal_ref,
    sibling_ref,
    message_ref,
    owned_ref,
    wide_ref,
    back_ref,
    reply_ref,
    replied_ref,
    mine_ref,
    other_ref,
    inverted_ref,
    samples_ref,
    load_sem,
    store_sem,
    lon_send,
    lon_recv,
    core_send,
    core_recv,
    out_send,
    out_recv,
    back_send,
    back_recv,
    grid_send,
    grid_recv,
    halo_send,
    halo_recv,
):
    a = lax.axis_index("lat")
    o = lax.axis_index("lon")
    core = lax.rem(o, 2)
    chip = a * (LONS // 2) + lax.div(o, 2)
    sibling = (a, o + 1 - 2 * core)

    def lon_at(step):
        return lax.rem(o + step, LONS)

    def chip_at(step):
        return lax.rem(chip + step, CHIPS)

    def chip_device(step):
        other = chip_at(step)
        return (lax.div(other, LONS // 2), 2 * lax.rem(other, LONS // 2) + core)

    def each(count, action):
        def step(s, carry):
            action(s)
            return carry

        lax.fori_loop(1, count, step, 0)

    def load_states(b):
        return pltpu.make_async_copy(
            states_hbm.at[:, pl.ds(pl.multiple_of(b * BLOCK, BLOCK), BLOCK)],
            states_ref.at[b],
            load_sem.at[b],
        )

    load_blocks = pltpu.make_async_copy(blocks_hbm, blocks_ref, load_sem.at[RES // BLOCK])

    barrier = pltpu.get_barrier_semaphore()
    each(
        LONS,
        lambda s: pl.semaphore_signal(
            barrier, inc=1, device_id=(a, lon_at(s)), device_id_type=MESH
        ),
    )
    each(
        CHIPS,
        lambda s: pl.semaphore_signal(
            barrier, inc=1, device_id=chip_device(s), device_id_type=MESH
        ),
    )
    load_blocks.start()
    each(RES // BLOCK, lambda b: load_states(b).start())
    load_states(0).start()
    halo_ref[...] = jnp.zeros_like(halo_ref)
    for d in range(LONS):
        sent_ref[d] = fields_ref[d * 144 : (d + 1) * 144, :].astype(jnp.bfloat16)
    pl.semaphore_wait(barrier, LONS + CHIPS - 2)

    def row_copy(s):
        return pltpu.make_async_remote_copy(
            src_ref=sent_ref.at[lon_at(s)],
            dst_ref=rows_ref.at[o],
            send_sem=lon_send.at[s],
            recv_sem=lon_recv.at[s],
            device_id=(a, lon_at(s)),
            device_id_type=MESH,
        )

    each(LONS, lambda s: row_copy(s).start())
    rows_ref[o] = sent_ref[o]

    entry = lax.broadcasted_iota(jnp.int32, (2 * WAVES, 2 * WAVES), 1)
    chosen = jnp.where(entry == column_ref[...], 1.0, 0.0).astype(jnp.bfloat16)
    for half, source in enumerate((forward_high_ref, forward_low_ref)):
        table_ref[half] = jnp.dot(
            chosen, source[...], preferred_element_type=jnp.float32
        ).astype(jnp.bfloat16)

    level = lax.broadcasted_iota(jnp.int32, (WAVES, CHANNELS), 0).astype(jnp.float32)
    cos_col = cos_ref[...]
    poles = []
    for s in range(2):
        m = slots_ref[2 * (a * LONS + o) + s]
        order = m.astype(jnp.float32)
        above = level > order
        order_sq = order * order
        prior = level - 1.0
        factor = jnp.sqrt(
            jnp.where(above, 4.0 * level * level - 1.0, 0.0)
            / jnp.where(above, level * level - order_sq, 1.0)
        )
        factor_ref[s, 0] = factor
        factor_ref[s, 1] = factor * jnp.sqrt(
            jnp.where(above, prior * prior - order_sq, 0.0)
            / jnp.where(level > 1.5, 4.0 * prior * prior - 1.0, 1.0)
        )
        factor_ref[s, 2] = jnp.where(level == order, 1.0, 0.0)
        index = lax.broadcasted_iota(jnp.int32, (1, WAVES), 1)
        logs = jnp.sum(jnp.where(index <= m, logs_ref[...], 0.0), axis=1, keepdims=True)
        poles.append(
            jnp.exp(0.5 * logs + order * log_sin_ref[...] - 0.5 * math.log(2.0))
        )

    def eight(base, carry):
        state = list(carry)
        at = pl.ds(pl.multiple_of(base * 8, 8), 8)
        for s in range(2):
            previous, current = state[s]
            factors = [factor_ref[s, f, at, :] for f in range(3)]
            stacked = []
            for step in range(8):
                row, drop, first = [
                    jnp.concatenate([f[step : step + 1]] * SUB_ROWS, axis=1) for f in factors
                ]
                value = row * (cos_col * current) - drop * previous + first * poles[s]
                previous, current = current, value
                stacked.append(value)
            state[s] = (previous, current)
            legendre_ref[s, at, :] = jnp.concatenate(stacked, axis=0)
        return tuple(state)

    zero = jnp.zeros((1, ROWS), jnp.float32)
    lax.fori_loop(0, WAVES // 8, eight, ((zero, zero), (zero, zero)))
    for s in range(2):
        table = legendre_ref[s]
        plain_ref[s] = table.astype(jnp.bfloat16)
        table = table * weight_ref[...]
        high = table.astype(jnp.bfloat16)
        weighted_ref[0, s] = high
        weighted_ref[1, s] = (table - high.astype(jnp.float32)).astype(jnp.bfloat16)

    def recur_blocks(part, first, last):
        def one(g, carry):
            left = jnp.concatenate(
                [states_ref[index_ref[g, l]] for l in range(CONN)],
                axis=1,
            )
            right = jnp.concatenate([blocks_ref[g, l] for l in range(CONN)], axis=1)
            recur_ref[:, pl.ds(pl.multiple_of(g * BLOCK, BLOCK), BLOCK)] = lax.dot_general(
                left, right, (((1,), (1,)), ((), ())), preferred_element_type=jnp.float32
            )
            return carry

        lax.fori_loop(first, last, one, 0)
        columns = pl.ds(first * BLOCK, (last - first) * BLOCK)
        copy = pltpu.make_async_copy(
            recur_ref.at[:, columns], recur_hbm.at[:, columns], store_sem.at[part]
        )
        copy.start()
        return copy

    load_states(0).wait()
    each(RES // BLOCK, lambda b: load_states(b).wait())
    load_blocks.wait()
    stores = [recur_blocks(0, 0, SPLIT[0])]
    each(LONS, lambda s: row_copy(s).wait_recv())

    data = rows_ref[...].reshape(LONS, SUB_ROWS, BAND, CHANNELS)
    data = jnp.concatenate(
        [data[:, r].reshape(COLS, CHANNELS) for r in range(SUB_ROWS)], axis=1
    )

    def transform(part):
        at = pl.ds(pl.multiple_of(part * WAVES, WAVES), WAVES)
        return jnp.dot(
            table_ref[0, at, :], data, preferred_element_type=jnp.float32
        ) + jnp.dot(table_ref[1, at, :], data, preferred_element_type=jnp.float32)

    zonal_ref[...] = transform(1 - core).astype(jnp.bfloat16)
    to_sibling = pltpu.make_async_remote_copy(
        src_ref=zonal_ref,
        dst_ref=sibling_ref,
        send_sem=core_send.at[0],
        recv_sem=core_recv.at[0],
        device_id=sibling,
        device_id_type=MESH,
    )
    to_sibling.start()
    own = transform(core)
    to_sibling.wait_recv()
    got = sibling_ref[...].astype(jnp.float32)
    lower = jnp.where(core == 0, own, got).reshape(CHIPS, 4, LANES)
    upper = jnp.where(core == 0, got, own).reshape(CHIPS, 4, LANES)
    message_ref[...] = jnp.concatenate([lower, upper], axis=1).astype(jnp.bfloat16)

    def out_copy(s):
        return pltpu.make_async_remote_copy(
            src_ref=message_ref.at[chip_at(s)],
            dst_ref=owned_ref.at[chip],
            send_sem=out_send.at[s],
            recv_sem=out_recv.at[s],
            device_id=chip_device(s),
            device_id_type=MESH,
        )

    each(CHIPS, lambda s: out_copy(s).start())
    owned_ref[chip] = message_ref[chip]

    entry = lax.broadcasted_iota(jnp.int32, (2 * WAVES, WAVES), 0)
    for half in range(2):
        chosen = jnp.where(
            entry == row_ref[:, half * WAVES : (half + 1) * WAVES], 1.0, 0.0
        ).astype(jnp.bfloat16)
        inverted_ref[half] = jnp.dot(
            inverse_ref[...], chosen, preferred_element_type=jnp.float32
        ).astype(jnp.bfloat16)
    stores.append(recur_blocks(1, SPLIT[0], SPLIT[1]))
    each(CHIPS, lambda s: out_copy(s).wait_recv())

    for r in range(SUB_ROWS):
        wide_ref[r] = (
            owned_ref[:, :, r * 128 : (r + 1) * 128]
            .astype(jnp.float32)
            .reshape(CHIPS * 8, CHANNELS)
        )
    scaled = level * (level + 1.0) / float((WAVES - 1) * WAVES)
    damping = 1.0 / (1.0 + diffusion_ref[...] * (scaled * scaled))
    damping = jnp.concatenate([damping, damping], axis=1)
    for s in range(2):
        zonal = jnp.concatenate(
            [
                jnp.concatenate(
                    [
                        wide_ref[r, pl.ds(4 * h + 2 * s + p, CHIPS, stride=8), :]
                        for r in range(SUB_ROWS)
                        for h in range(2)
                    ],
                    axis=0,
                )
                for p in range(2)
            ],
            axis=1,
        ).astype(jnp.bfloat16)
        filtered = damping * (
            jnp.dot(weighted_ref[0, s], zonal, preferred_element_type=jnp.float32)
            + jnp.dot(weighted_ref[1, s], zonal, preferred_element_type=jnp.float32)
        )
        for p in range(2):
            spectral_ref[s, p] = filtered[:, p * 128 : (p + 1) * 128]
        grid = lax.dot_general(
            plain_ref[s],
            filtered.astype(jnp.bfloat16),
            (((0,), (0,)), ((), ())),
            preferred_element_type=jnp.float32,
        )
        for p in range(2):
            for r in range(SUB_ROWS):
                for h in range(2):
                    at = r * 128 + h * CHIPS
                    back_ref[r, pl.ds(4 * h + 2 * s + p, CHIPS, stride=8), :] = grid[
                        at : at + CHIPS, p * 128 : (p + 1) * 128
                    ]
    for r in range(SUB_ROWS):
        reply_ref[:, :, r * 128 : (r + 1) * 128] = (
            back_ref[r].reshape(CHIPS, 8, CHANNELS).astype(jnp.bfloat16)
        )

    def back_copy(s):
        return pltpu.make_async_remote_copy(
            src_ref=reply_ref.at[chip_at(s)],
            dst_ref=replied_ref.at[chip],
            send_sem=back_send.at[s],
            recv_sem=back_recv.at[s],
            device_id=chip_device(s),
            device_id_type=MESH,
        )

    each(CHIPS, lambda s: back_copy(s).start())
    replied_ref[chip] = reply_ref[chip]
    stores.append(recur_blocks(2, SPLIT[1], SPLIT[2]))
    each(CHIPS, lambda s: back_copy(s).wait_recv())

    whole = replied_ref[...].astype(jnp.float32)
    lower = whole[:, 0:4].reshape(2 * CHIPS * 2, LANES)
    upper = whole[:, 4:8].reshape(2 * CHIPS * 2, LANES)
    other_ref[...] = jnp.where(core == 0, upper, lower).astype(jnp.bfloat16)
    for_sibling = pltpu.make_async_remote_copy(
        src_ref=other_ref,
        dst_ref=mine_ref,
        send_sem=core_send.at[1],
        recv_sem=core_recv.at[1],
        device_id=sibling,
        device_id_type=MESH,
    )
    for_sibling.start()
    kept = jnp.where(core == 0, lower, upper).astype(jnp.bfloat16)
    own = jnp.dot(inverted_ref[core], kept, preferred_element_type=jnp.float32)
    for_sibling.wait_recv()
    own += jnp.dot(inverted_ref[1 - core], mine_ref[...], preferred_element_type=jnp.float32)
    for d in range(LONS):
        samples_ref[d] = own[d * SENT_COLS : (d + 1) * SENT_COLS].astype(jnp.bfloat16)

    def grid_copy(s):
        return pltpu.make_async_remote_copy(
            src_ref=samples_ref.at[lon_at(s)],
            dst_ref=framed_ref.at[o],
            send_sem=grid_send.at[s],
            recv_sem=grid_recv.at[s],
            device_id=(a, lon_at(s)),
            device_id_type=MESH,
        )

    each(LONS, lambda s: grid_copy(s).start())
    framed_ref[o] = samples_ref[o]
    stores.append(recur_blocks(3, SPLIT[2], SPLIT[3]))
    each(LONS, lambda s: grid_copy(s).wait_recv())

    up = pltpu.make_async_remote_copy(
        src_ref=framed_ref.at[LONS - 1, :, pl.ds(CHANNELS, 2 * CHANNELS)],
        dst_ref=halo_ref.at[0],
        send_sem=halo_send.at[0],
        recv_sem=halo_recv.at[0],
        device_id=(lax.rem(a + 1, LATS), o),
        device_id_type=MESH,
    )
    down = pltpu.make_async_remote_copy(
        src_ref=framed_ref.at[0, :, pl.ds(0, 2 * CHANNELS)],
        dst_ref=halo_ref.at[1],
        send_sem=halo_send.at[1],
        recv_sem=halo_recv.at[1],
        device_id=(lax.rem(a + LATS - 1, LATS), o),
        device_id_type=MESH,
    )

    @pl.when(a < LATS - 1)
    def _():
        up.start()

    @pl.when(a > 0)
    def _():
        down.start()

    each(LONS, lambda s: row_copy(s).wait_send())
    each(CHIPS, lambda s: out_copy(s).wait_send())
    each(CHIPS, lambda s: back_copy(s).wait_send())
    each(LONS, lambda s: grid_copy(s).wait_send())
    to_sibling.wait_send()
    for_sibling.wait_send()
    for copy in stores:
        copy.wait()

    @pl.when(a < LATS - 1)
    def _():
        up.wait_send()
        down.wait_recv()

    @pl.when(a > 0)
    def _():
        down.wait_send()
        up.wait_recv()


def reservoir_kernel(
    rows_ref,
    halo_ref,
    recur_ref,
    node_ref,
    gain_ref,
    readout_ref,
    blend_ref,
    next_ref,
    frame_ref,
    drive_ref,
    total_ref,
):
    chunk = pl.program_id(0)

    @pl.when(chunk == 0)
    def _():
        def row_of(position):
            if position < 2:
                part = halo_ref[0, :, position * 128 : (position + 1) * 128]
            elif position >= BAND + 2:
                at = position - BAND - 2
                part = halo_ref[1, :, at * 128 : (at + 1) * 128]
            else:
                j = position - 2
                at = j % SUB_ROWS
                part = rows_ref[j // SUB_ROWS, :, at * 128 : (at + 1) * 128]
            return part.astype(jnp.float32)

        for pair in range(FRAME // 2):
            for a in range(2):
                upper = row_of(4 * pair + a)
                lower = row_of(4 * pair + 2 + a)
                for b in range(WINDOW):
                    start = (b % 2) * HALF + b // 2
                    both = jnp.concatenate(
                        [upper[start : start + TILES], lower[start : start + TILES]], axis=0
                    )
                    at = (b * 2 + a) * 128
                    frame_ref[pair * 48 : (pair + 1) * 48, at : at + 128] = both.astype(
                        jnp.bfloat16
                    )
        total_ref[...] = jnp.zeros_like(total_ref)

    entry = lax.broadcasted_iota(jnp.int32, (PICK, CHUNK), 0)
    pick = jnp.where(entry == node_ref[1:2, :], 1.0, 0.0).astype(jnp.bfloat16)
    drive_ref[...] = jnp.dot(frame_ref[...], pick, preferred_element_type=jnp.float32)
    count = TILES * TILES
    row = node_ref[0:1, :]
    picked = jnp.where(
        row == 0,
        drive_ref[0:count],
        jnp.where(row == 1, drive_ref[TILES : count + TILES], drive_ref[2 * TILES :]),
    )
    upcoming = jnp.tanh(recur_ref[...] + picked * gain_ref[0:1, :] + gain_ref[1:2, :]).astype(
        jnp.bfloat16
    )
    next_ref[...] = upcoming
    total_ref[...] += jnp.dot(upcoming, readout_ref[...], preferred_element_type=jnp.float32)

    @pl.when(chunk == CHUNKS - 1)
    def _():
        for a in range(2):
            for b in range(2):
                at = ((2 + b) * 2 + a) * 128
                forecast = frame_ref[:, at : at + 128].astype(jnp.float32)
                to = (a * 2 + b) * 128
                for i in range(TILES):
                    blend_ref[pl.ds((2 * i + a) * BAND + b, TILES, stride=2), :] = (
                        forecast[(i + 1) * TILES : (i + 2) * TILES]
                        + total_ref[i * TILES : (i + 1) * TILES, to : to + 128]
                    )


def shards(
    fields,
    diffusion,
    wave_slots,
    reservoir_state,
    adjacency_blocks,
    adjacency_index,
    input_index,
    input_gain,
    bias,
    readout,
):
    vmem = pl.BlockSpec(memory_space=pltpu.VMEM)
    smem = pl.BlockSpec(memory_space=pltpu.SMEM)
    hbm = pl.BlockSpec(memory_space=pl.ANY)
    bf16 = functools.partial(pltpu.VMEM, dtype=jnp.bfloat16)
    f32 = functools.partial(pltpu.VMEM, dtype=jnp.float32)

    order = wave_slots.reshape(CHIPS, 2, 2).transpose(1, 0, 2).reshape(-1, 1)
    slot_part = (2 * order + jnp.arange(2, dtype=jnp.int32)).reshape(-1)
    forward_high, forward_low = split(forward_rows().astype(np.float32))
    cos_col, sin_col = geometry()
    spectral, framed, halo, recur = pl.pallas_call(
        chain_kernel,
        out_shape=(
            jax.ShapeDtypeStruct((2, 2, WAVES, CHANNELS), jnp.float32),
            jax.ShapeDtypeStruct((LONS, SENT_COLS, LANES), jnp.bfloat16),
            jax.ShapeDtypeStruct((2, SENT_COLS, 2 * CHANNELS), jnp.bfloat16),
            jax.ShapeDtypeStruct((NODES, RES), jnp.float32),
        ),
        in_specs=[smem] * 2 + [vmem] * 11 + [hbm] * 2,
        out_specs=(vmem, vmem, vmem, hbm),
        scratch_shapes=[
            bf16((RES // BLOCK, NODES, BLOCK)),
            bf16((RES // BLOCK, CONN, BLOCK, BLOCK)),
            f32((NODES, RES)),
            bf16((LONS, SUB_ROWS * BAND, CHANNELS)),
            bf16((LONS, SUB_ROWS * BAND, CHANNELS)),
            bf16((2, 2 * WAVES, COLS)),
            f32((2, 3, WAVES, CHANNELS)),
            f32((2, WAVES, ROWS)),
            bf16((2, 2, WAVES, ROWS)),
            bf16((2, WAVES, ROWS)),
            bf16((WAVES, LANES)),
            bf16((WAVES, LANES)),
            bf16((CHIPS, 8, LANES)),
            bf16((CHIPS, 8, LANES)),
            f32((SUB_ROWS, 8 * CHIPS, CHANNELS)),
            f32((SUB_ROWS, 8 * CHIPS, CHANNELS)),
            bf16((CHIPS, 8, LANES)),
            bf16((CHIPS, 8, LANES)),
            bf16((WAVES, LANES)),
            bf16((WAVES, LANES)),
            bf16((2, LONS * SENT_COLS, WAVES)),
            bf16((LONS, SENT_COLS, LANES)),
            pltpu.SemaphoreType.DMA((RES // BLOCK + 1,)),
            pltpu.SemaphoreType.DMA((4,)),
            pltpu.SemaphoreType.DMA((LONS,)),
            pltpu.SemaphoreType.DMA((LONS,)),
            pltpu.SemaphoreType.DMA((2,)),
            pltpu.SemaphoreType.DMA((2,)),
            pltpu.SemaphoreType.DMA((CHIPS,)),
            pltpu.SemaphoreType.DMA((CHIPS,)),
            pltpu.SemaphoreType.DMA((CHIPS,)),
            pltpu.SemaphoreType.DMA((CHIPS,)),
            pltpu.SemaphoreType.DMA((LONS,)),
            pltpu.SemaphoreType.DMA((LONS,)),
            pltpu.SemaphoreType.DMA((2,)),
            pltpu.SemaphoreType.DMA((2,)),
        ],
        compiler_params=pltpu.CompilerParams(
            collective_id=0, has_side_effects=True, vmem_limit_bytes=56 * MB
        ),
        cost_estimate=pl.CostEstimate(
            flops=2 * NODES * RES * CONN * BLOCK, bytes_accessed=30 * MB, transcendentals=0
        ),
        name="chain",
    )(
        wave_slots,
        adjacency_index,
        fields.reshape(BAND * BAND, CHANNELS),
        slot_part[:, None],
        slot_part[None, :],
        jnp.asarray(forward_high),
        jnp.asarray(forward_low),
        jnp.asarray(inverse_columns(), jnp.bfloat16),
        jnp.asarray(cos_col[None, :], jnp.float32),
        jnp.asarray(np.log(sin_col)[None, :], jnp.float32),
        jnp.asarray((math.pi / ROWS) * sin_col[None, :], jnp.float32),
        diffusion[None, :],
        jnp.asarray(log_terms()[None, :], jnp.float32),
        reservoir_state.reshape(NODES, RES),
        adjacency_blocks,
    )

    row_at = input_index // (WINDOW * CHANNELS)
    col_at = input_index // CHANNELS % WINDOW
    key = (col_at * 2 + row_at % 2) * CHANNELS + input_index % CHANNELS
    const = lambda *zeros: (lambda c: zeros)
    blended, upcoming = pl.pallas_call(
        reservoir_kernel,
        grid=(CHUNKS,),
        out_shape=(
            jax.ShapeDtypeStruct((BAND * BAND, CHANNELS), jnp.float32),
            jax.ShapeDtypeStruct((NODES, RES), jnp.bfloat16),
        ),
        in_specs=[
            pl.BlockSpec((LONS, SENT_COLS, LANES), const(0, 0, 0)),
            pl.BlockSpec((2, SENT_COLS, 2 * CHANNELS), const(0, 0, 0)),
            pl.BlockSpec((NODES, CHUNK), lambda c: (0, c)),
            pl.BlockSpec((2, CHUNK), lambda c: (0, c)),
            pl.BlockSpec((2, CHUNK), lambda c: (0, c)),
            pl.BlockSpec((CHUNK, 4 * CHANNELS), lambda c: (c, 0)),
        ],
        out_specs=(
            pl.BlockSpec((BAND * BAND, CHANNELS), const(0, 0)),
            pl.BlockSpec((NODES, CHUNK), lambda c: (0, c)),
        ),
        scratch_shapes=[
            pltpu.VMEM((FRAME * TILES, PICK), jnp.bfloat16),
            pltpu.VMEM((FRAME * TILES, CHUNK), jnp.float32),
            pltpu.VMEM((NODES, 4 * CHANNELS), jnp.float32),
        ],
        compiler_params=pltpu.CompilerParams(vmem_limit_bytes=56 * MB),
        cost_estimate=pl.CostEstimate(
            flops=2 * FRAME * TILES * RES * PICK,
            bytes_accessed=24 * MB,
            transcendentals=NODES * RES,
        ),
        name="reservoir",
    )(
        framed,
        halo,
        recur,
        jnp.stack([row_at // 2, key]),
        jnp.stack([input_gain, bias]),
        readout,
    )
    return (
        blended.reshape(BAND, BAND, CHANNELS),
        upcoming.reshape(TILES, TILES, RES),
        spectral,
    )


def solution(mesh):
    placed = (P("lat", "lon", None), P(), P(), P("lat", "lon", None), P(), P(), P(), P(), P(), P())
    return jax.shard_map(
        shards,
        mesh=mesh,
        in_specs=placed,
        out_specs=(
            P("lat", "lon", None),
            P("lat", "lon", None),
            P(("lat", "lon"), None, None, None),
        ),
        check_vma=False,
    )
```

time: 139 us -> 86.2 us (0.62)
  the two profiles are of different devices: /device:TPU:40 before, /device:TPU:1 now
where the time goes in v1:
time: 86.2 us; the launch traced here: 85.7 us
  Pallas kernels  77.5 us (90%)
  local copies, waits for them, and re-layouts  4 us (5%)
  other arithmetic  3.55 us (4%)
    pallas_call x1, Pallas kernels, shards(): pl.pallas_call(chain_kernel, out_shape=(jax.ShapeDtypeStruct((2, 2, WAVES...  60.9 us
    pallas_call x1, Pallas kernels, shards(): pl.pallas_call(reservoir_kernel, grid=(CHUNKS,), out_shape=(jax.ShapeDtyp...  16.6 us
    unnamed x4, local copies, waits for them, and re-layouts  2.16 us

profile of v1, /device:TPU:1, one launch (start us, length us, event | category | flops | bytes accessed | tf_op | source)
XLA Modules:
  0.0 85.7 jit_solution(520486293931161481)
XLA Ops:
  0.6 0.7 broadcast_multiply_fusion
  1.3 1.4 %copy.22.index_ref = s32[32,8]{1,0:T(8,128)} copy(s32[32,8]{0,1:T(8,128)} %param.22) | data formatting | bytes 2048 | tf_op args[5]
  2.7 1.4 %pad_maximum_fusion.gain_ref = f32[2,4096]{1,0:T(2,128)} fusion(f32[1,4096]{1,0:T(1,128)} %bitcast.13, f32[1,4096]{1,0:T(1,128)} %bitcast.14), kind=kLoop, calls=%fused_computation.2 | loop fusion | flops 8192 | bytes 65536 | tf_op jit(solution)/shard_map/stack | solution.py:690
  4.0 0.8 add_select_fusion.4
  4.8 0.6 pad_add_fusion.node_ref
  5.4 0.2 mul.30
  5.6 0.1 mul.32
  5.8 0.1 iota_add_fusion
  5.9 0.7 add.60.row_ref
  6.6 0.8 add.66.column_ref
  7.4 60.9 %chain.1 = (f32[2,2,256,128]{3,2,1,0:T(8,128)}, bf16[16,56,384]{2,1,0:T(8,128)(2,1)}, bf16[2,56,256]{2,1,0:T(8,128)(2,1)}, f32[576,4096]{1,0:T(8,128)}) custom-call(s32[256]{0:T(256)} %slots_ref.1, s32[32,8]{1,0:T(8,128)} %copy.22.index_ref, f32[2304,128]{1,0:T(8,128)} %bitcast.16, s32[512,1]{1,0:T(8,128)} %add.66.column_ref, s32[1,512]{1,0:T(1,128)} %add.60.row_ref, ...), custom_call_target="tpu_custom_call" | custom-call | flops 4831838208 | bytes 31457280 | tf_op jit(solution)/shard_map/chain/pallas_call | solution.py:577
  68.3 0.0 copy-start
  68.3 16.6 %reservoir.1 = (f32[2304,128]{1,0:T(8,128)}, bf16[576,4096]{1,0:T(8,128)(2,1)}) custom-call(bf16[16,56,384]{2,1,0:T(8,128)(2,1)} %get-tuple-element.9.rows_ref, bf16[2,56,256]{2,1,0:T(8,128)(2,1)} %get-tuple-element.10.halo_ref, f32[576,4096]{1,0:T(8,128)} %get-tuple-element.11.recur_ref, s32[2,4096]{1,0:T(2,128)} %pad_add_fusion.node_ref, ...), custom_call_target="tpu_custom_call" | custom-call | flops 7851737088 | bytes 25165824 | tf_op jit(solution)/shard_map/reservoir/pallas_call | solution.py:654
  84.9 0.0 copy-done
  84.9 0.8 copy.25
  (1 shorter events, 0.0 us)
Async XLA Ops:
  68.3 16.6 %copy-start = (f32[2,2,256,128]{3,2,1,0:T(8,128)S(1)}, f32[2,2,256,128]{3,2,1,0:T(8,128)}, u32[]{:S(2)}) copy-start(f32[2,2,256,128]{3,2,1,0:T(8,128)} %get-tuple-element.22) | copy-start | bytes 1572868

commit v2 on v1

--- a/solution.py
+++ b/solution.py
@@ -30,7 +30,7 @@
 FRAME = TILES + 2
 CHUNK = 512
 CHUNKS = RES // CHUNK
-PICK = 2 * WINDOW * CHANNELS
+FRAME_ROWS = 736
 MB = 1 << 20
 MESH = pl.DeviceIdType.MESH
 SPLIT = (7, 16, 24, 32)
@@ -78,8 +78,7 @@
     slots_ref,
     index_ref,
     fields_ref,
-    column_ref,
-    row_ref,
+    order_ref,
     forward_high_ref,
     forward_low_ref,
     inverse_ref,
@@ -99,6 +98,7 @@
     recur_ref,
     sent_ref,
     rows_ref,
+    chosen_ref,
     table_ref,
     factor_ref,
     legendre_ref,
@@ -137,11 +137,24 @@
     chip = a * (LONS // 2) + lax.div(o, 2)
     sibling = (a, o + 1 - 2 * core)
 
+    def along(digit):
+        half = lax.div(digit, 2)
+        return (1 - half) * (2 - digit) + half * 3 * (3 - digit)
+
+    def moved(at, size, by):
+        return lax.rem(at + by, size)
+
     def lon_at(step):
-        return lax.rem(o + step, LONS)
+        z = moved(lax.div(o, 8), 2, 1 - lax.div(step, 8))
+        y = moved(lax.rem(lax.div(o, 2), 4), 4, along(lax.rem(lax.div(step, 2), 4)))
+        return z * 8 + y * 2 + moved(core, 2, 1 - lax.rem(step, 2))
 
     def chip_at(step):
-        return lax.rem(chip + step, CHIPS)
+        z_hi = moved(lax.div(o, 8), 2, 1 - lax.div(step, 32))
+        x = moved(lax.rem(a, 4), 4, along(lax.rem(lax.div(step, 8), 4)))
+        y = moved(lax.rem(lax.div(o, 2), 4), 4, along(lax.rem(lax.div(step, 2), 4)))
+        z_lo = moved(lax.div(a, 4), 2, 1 - lax.rem(step, 2))
+        return (z_lo * 4 + x) * 8 + z_hi * 4 + y
 
     def chip_device(step):
         other = chip_at(step)
@@ -152,7 +165,7 @@
             action(s)
             return carry
 
-        lax.fori_loop(1, count, step, 0)
+        lax.fori_loop(0, count - 1, step, 0)
 
     def load_states(b):
         return pltpu.make_async_copy(
@@ -165,20 +178,19 @@
 
     barrier = pltpu.get_barrier_semaphore()
     each(
+        CHIPS,
+        lambda s: pl.semaphore_signal(
+            barrier, inc=1, device_id=chip_device(s), device_id_type=MESH
+        ),
+    )
+    each(
         LONS,
         lambda s: pl.semaphore_signal(
             barrier, inc=1, device_id=(a, lon_at(s)), device_id_type=MESH
         ),
     )
-    each(
-        CHIPS,
-        lambda s: pl.semaphore_signal(
-            barrier, inc=1, device_id=chip_device(s), device_id_type=MESH
-        ),
-    )
     load_blocks.start()
-    each(RES // BLOCK, lambda b: load_states(b).start())
-    load_states(0).start()
+    each(RES // BLOCK + 1, lambda b: load_states(b).start())
     halo_ref[...] = jnp.zeros_like(halo_ref)
     for d in range(LONS):
         sent_ref[d] = fields_ref[d * 144 : (d + 1) * 144, :].astype(jnp.bfloat16)
@@ -197,11 +209,24 @@
     each(LONS, lambda s: row_copy(s).start())
     rows_ref[o] = sent_ref[o]
 
-    entry = lax.broadcasted_iota(jnp.int32, (2 * WAVES, 2 * WAVES), 1)
-    chosen = jnp.where(entry == column_ref[...], 1.0, 0.0).astype(jnp.bfloat16)
+    column = lax.broadcasted_iota(jnp.int32, (WAVES, 2 * WAVES), 1)
+    slot = 4 * ((column >> 2) & (CHIPS - 1)) + 2 * (column >> 8) + ((column >> 1) & 1)
+    moves = jnp.where(lax.broadcasted_iota(jnp.int32, slot.shape, 0) == slot, 1.0, 0.0)
+    waves = jnp.broadcast_to(order_ref[...].astype(jnp.float32), (8, WAVES))
+    waves = jnp.dot(
+        waves.astype(jnp.bfloat16),
+        moves.astype(jnp.bfloat16),
+        preferred_element_type=jnp.float32,
+    ).astype(jnp.int32)
+    key = 2 * waves[0:1] + (column[0:1] & 1)
+    entry = lax.broadcasted_iota(jnp.int32, (2 * WAVES, 2 * WAVES), 0)
+    chosen_ref[...] = jnp.where(entry == key, 1.0, 0.0).astype(jnp.bfloat16)
     for half, source in enumerate((forward_high_ref, forward_low_ref)):
-        table_ref[half] = jnp.dot(
-            chosen, source[...], preferred_element_type=jnp.float32
+        table_ref[half] = lax.dot_general(
+            chosen_ref[...],
+            source[...],
+            (((0,), (0,)), ((), ())),
+            preferred_element_type=jnp.float32,
         ).astype(jnp.bfloat16)
 
     level = lax.broadcasted_iota(jnp.int32, (WAVES, CHANNELS), 0).astype(jnp.float32)
@@ -260,7 +285,7 @@
     def recur_blocks(part, first, last):
         def one(g, carry):
             left = jnp.concatenate(
-                [states_ref[index_ref[g, l]] for l in range(CONN)],
+                [states_ref[index_ref[l, g]] for l in range(CONN)],
                 axis=1,
             )
             right = jnp.concatenate([blocks_ref[g, l] for l in range(CONN)], axis=1)
@@ -277,8 +302,7 @@
         copy.start()
         return copy
 
-    load_states(0).wait()
-    each(RES // BLOCK, lambda b: load_states(b).wait())
+    each(RES // BLOCK + 1, lambda b: load_states(b).wait())
     load_blocks.wait()
     stores = [recur_blocks(0, 0, SPLIT[0])]
     each(LONS, lambda s: row_copy(s).wait_recv())
@@ -324,13 +348,11 @@
     each(CHIPS, lambda s: out_copy(s).start())
     owned_ref[chip] = message_ref[chip]
 
-    entry = lax.broadcasted_iota(jnp.int32, (2 * WAVES, WAVES), 0)
     for half in range(2):
-        chosen = jnp.where(
-            entry == row_ref[:, half * WAVES : (half + 1) * WAVES], 1.0, 0.0
-        ).astype(jnp.bfloat16)
         inverted_ref[half] = jnp.dot(
-            inverse_ref[...], chosen, preferred_element_type=jnp.float32
+            inverse_ref[...],
+            chosen_ref[:, half * WAVES : (half + 1) * WAVES],
+            preferred_element_type=jnp.float32,
         ).astype(jnp.bfloat16)
     stores.append(recur_blocks(1, SPLIT[0], SPLIT[1]))
     each(CHIPS, lambda s: out_copy(s).wait_recv())
@@ -423,16 +445,24 @@
             src_ref=samples_ref.at[lon_at(s)],
             dst_ref=framed_ref.at[o],
             send_sem=grid_send.at[s],
-            recv_sem=grid_recv.at[s],
+            recv_sem=grid_recv.at[o],
             device_id=(a, lon_at(s)),
+            device_id_type=MESH,
+        )
+
+    def grid_from(source):
+        return pltpu.make_async_remote_copy(
+            src_ref=samples_ref.at[source],
+            dst_ref=framed_ref.at[source],
+            send_sem=grid_send.at[LONS - 1],
+            recv_sem=grid_recv.at[source],
+            device_id=(a, source),
             device_id_type=MESH,
         )
 
     each(LONS, lambda s: grid_copy(s).start())
     framed_ref[o] = samples_ref[o]
     stores.append(recur_blocks(3, SPLIT[2], SPLIT[3]))
-    each(LONS, lambda s: grid_copy(s).wait_recv())
-
     up = pltpu.make_async_remote_copy(
         src_ref=framed_ref.at[LONS - 1, :, pl.ds(CHANNELS, 2 * CHANNELS)],
         dst_ref=halo_ref.at[0],
@@ -450,14 +480,30 @@
         device_id_type=MESH,
     )
 
+    @pl.when(o < LONS - 1)
+    def _():
+        grid_from(LONS - 1).wait_recv()
+
     @pl.when(a < LATS - 1)
     def _():
         up.start()
 
+    @pl.when(o > 0)
+    def _():
+        grid_from(0).wait_recv()
+
     @pl.when(a > 0)
     def _():
         down.start()
 
+    def arrived(source, carry):
+        @pl.when(source != o)
+        def _():
+            grid_from(source).wait_recv()
+
+        return carry
+
+    lax.fori_loop(1, LONS - 1, arrived, 0)
     each(LONS, lambda s: row_copy(s).wait_send())
     each(CHIPS, lambda s: out_copy(s).wait_send())
     each(CHIPS, lambda s: back_copy(s).wait_send())
@@ -482,16 +528,20 @@
     rows_ref,
     halo_ref,
     recur_ref,
-    node_ref,
+    entry_ref,
     gain_ref,
+    bias_ref,
     readout_ref,
+    coefficients_ref,
     blend_ref,
     next_ref,
+    spectral_ref,
     frame_ref,
     drive_ref,
     total_ref,
 ):
     chunk = pl.program_id(0)
+    spectral_ref[...] = coefficients_ref[...]
 
     @pl.when(chunk == 0)
     def _():
@@ -507,48 +557,72 @@
                 part = rows_ref[j // SUB_ROWS, :, at * 128 : (at + 1) * 128]
             return part.astype(jnp.float32)
 
-        for pair in range(FRAME // 2):
+        for group in range(0, FRAME, 4):
             for a in range(2):
-                upper = row_of(4 * pair + a)
-                lower = row_of(4 * pair + 2 + a)
-                for b in range(WINDOW):
-                    start = (b % 2) * HALF + b // 2
-                    both = jnp.concatenate(
-                        [upper[start : start + TILES], lower[start : start + TILES]], axis=0
-                    )
-                    at = (b * 2 + a) * 128
-                    frame_ref[pair * 48 : (pair + 1) * 48, at : at + 128] = both.astype(
-                        jnp.bfloat16
+                parts = [row_of(2 * i + a) for i in range(group, min(group + 4, FRAME))]
+                for b in range(2):
+                    block = [part[b * HALF : (b + 1) * HALF] for part in parts]
+                    if len(block) < 4:
+                        block.append(jnp.zeros((FRAME_ROWS - FRAME * HALF, CHANNELS), jnp.float32))
+                    block = jnp.concatenate(block, axis=0)
+                    at = (a * 2 + b) * 128
+                    frame_ref[group * HALF : group * HALF + block.shape[0], at : at + 128] = (
+                        block.astype(jnp.bfloat16)
                     )
         total_ref[...] = jnp.zeros_like(total_ref)
 
-    entry = lax.broadcasted_iota(jnp.int32, (PICK, CHUNK), 0)
-    pick = jnp.where(entry == node_ref[1:2, :], 1.0, 0.0).astype(jnp.bfloat16)
-    drive_ref[...] = jnp.dot(frame_ref[...], pick, preferred_element_type=jnp.float32)
-    count = TILES * TILES
-    row = node_ref[0:1, :]
-    picked = jnp.where(
-        row == 0,
-        drive_ref[0:count],
-        jnp.where(row == 1, drive_ref[TILES : count + TILES], drive_ref[2 * TILES :]),
-    )
-    upcoming = jnp.tanh(recur_ref[...] + picked * gain_ref[0:1, :] + gain_ref[1:2, :]).astype(
-        jnp.bfloat16
-    )
-    next_ref[...] = upcoming
-    total_ref[...] += jnp.dot(upcoming, readout_ref[...], preferred_element_type=jnp.float32)
+    index = entry_ref[...]
+    place = index >> 7
+    row_at = (place * 43) >> 8
+    col_at = place - WINDOW * row_at
+    key = ((row_at & 1) * 2 + (col_at & 1)) * CHANNELS + (index & (CHANNELS - 1))
+    pick = jnp.where(
+        lax.broadcasted_iota(jnp.int32, (4 * CHANNELS, CHUNK), 0) == key, 1.0, 0.0
+    ).astype(jnp.bfloat16)
+    drive = jnp.dot(frame_ref[...], pick, preferred_element_type=jnp.float32)
+    for q in range(CHUNK // 128):
+        drive_ref[q] = drive[:, q * 128 : (q + 1) * 128]
+    for q in range(CHUNK // 128):
+        lanes = slice(q * 128, (q + 1) * 128)
+        col = jnp.broadcast_to(col_at[:, lanes] >> 1, (TILES, 128))
+        row = jnp.broadcast_to(row_at[:, lanes] >> 1, (TILES, 128))
+        col_one, col_two = col == 1, col == 2
+        row_one, row_two = row == 1, row == 2
+        gain = gain_ref[:, lanes]
+        bias = bias_ref[:, lanes]
+
+        def shifted(i):
+            near, next_one, far = [
+                drive_ref[q, i * HALF + k : i * HALF + k + TILES, :] for k in range(3)
+            ]
+            return jnp.where(col_two, far, jnp.where(col_one, next_one, near))
+
+        kept = [shifted(0), shifted(1)]
+        for i in range(0, TILES, 2):
+            both = []
+            for step in range(2):
+                kept.append(shifted(i + step + 2))
+                near, next_one, far = kept
+                picked = jnp.where(row_two, far, jnp.where(row_one, next_one, near))
+                kept = kept[1:]
+                at = (i + step) * TILES
+                both.append(jnp.tanh(recur_ref[at : at + TILES, lanes] + picked * gain + bias))
+            next_ref[i * TILES : (i + 2) * TILES, lanes] = jnp.concatenate(both, axis=0).astype(
+                jnp.bfloat16
+            )
+    total_ref[...] += jnp.dot(next_ref[...], readout_ref[...], preferred_element_type=jnp.float32)
 
     @pl.when(chunk == CHUNKS - 1)
     def _():
         for a in range(2):
             for b in range(2):
-                at = ((2 + b) * 2 + a) * 128
+                at = (a * 2 + b) * 128
                 forecast = frame_ref[:, at : at + 128].astype(jnp.float32)
-                to = (a * 2 + b) * 128
                 for i in range(TILES):
+                    start = (i + 1) * HALF + 1
                     blend_ref[pl.ds((2 * i + a) * BAND + b, TILES, stride=2), :] = (
-                        forecast[(i + 1) * TILES : (i + 2) * TILES]
-                        + total_ref[i * TILES : (i + 1) * TILES, to : to + 128]
+                        forecast[start : start + TILES]
+                        + total_ref[i * TILES : (i + 1) * TILES, at : at + 128]
                     )
 
 
@@ -570,8 +644,6 @@
     bf16 = functools.partial(pltpu.VMEM, dtype=jnp.bfloat16)
     f32 = functools.partial(pltpu.VMEM, dtype=jnp.float32)
 
-    order = wave_slots.reshape(CHIPS, 2, 2).transpose(1, 0, 2).reshape(-1, 1)
-    slot_part = (2 * order + jnp.arange(2, dtype=jnp.int32)).reshape(-1)
     forward_high, forward_low = split(forward_rows().astype(np.float32))
     cos_col, sin_col = geometry()
     spectral, framed, halo, recur = pl.pallas_call(
@@ -582,7 +654,7 @@
             jax.ShapeDtypeStruct((2, SENT_COLS, 2 * CHANNELS), jnp.bfloat16),
             jax.ShapeDtypeStruct((NODES, RES), jnp.float32),
         ),
-        in_specs=[smem] * 2 + [vmem] * 11 + [hbm] * 2,
+        in_specs=[smem] * 2 + [vmem] * 10 + [hbm] * 2,
         out_specs=(vmem, vmem, vmem, hbm),
         scratch_shapes=[
             bf16((RES // BLOCK, NODES, BLOCK)),
@@ -590,6 +662,7 @@
             f32((NODES, RES)),
             bf16((LONS, SUB_ROWS * BAND, CHANNELS)),
             bf16((LONS, SUB_ROWS * BAND, CHANNELS)),
+            bf16((2 * WAVES, 2 * WAVES)),
             bf16((2, 2 * WAVES, COLS)),
             f32((2, 3, WAVES, CHANNELS)),
             f32((2, WAVES, ROWS)),
@@ -631,10 +704,9 @@
         name="chain",
     )(
         wave_slots,
-        adjacency_index,
+        adjacency_index.T,
         fields.reshape(BAND * BAND, CHANNELS),
-        slot_part[:, None],
-        slot_part[None, :],
+        wave_slots[None, :],
         jnp.asarray(forward_high),
         jnp.asarray(forward_low),
         jnp.asarray(inverse_columns(), jnp.bfloat16),
@@ -647,37 +719,38 @@
         adjacency_blocks,
     )
 
-    row_at = input_index // (WINDOW * CHANNELS)
-    col_at = input_index // CHANNELS % WINDOW
-    key = (col_at * 2 + row_at % 2) * CHANNELS + input_index % CHANNELS
     const = lambda *zeros: (lambda c: zeros)
-    blended, upcoming = pl.pallas_call(
+    blended, upcoming, spectral = pl.pallas_call(
         reservoir_kernel,
         grid=(CHUNKS,),
         out_shape=(
             jax.ShapeDtypeStruct((BAND * BAND, CHANNELS), jnp.float32),
             jax.ShapeDtypeStruct((NODES, RES), jnp.bfloat16),
+            jax.ShapeDtypeStruct((4 * WAVES, CHANNELS), jnp.float32),
         ),
         in_specs=[
             pl.BlockSpec((LONS, SENT_COLS, LANES), const(0, 0, 0)),
             pl.BlockSpec((2, SENT_COLS, 2 * CHANNELS), const(0, 0, 0)),
             pl.BlockSpec((NODES, CHUNK), lambda c: (0, c)),
-            pl.BlockSpec((2, CHUNK), lambda c: (0, c)),
-            pl.BlockSpec((2, CHUNK), lambda c: (0, c)),
+            pl.BlockSpec((1, CHUNK), lambda c: (0, c)),
+            pl.BlockSpec((1, CHUNK), lambda c: (0, c)),
+            pl.BlockSpec((1, CHUNK), lambda c: (0, c)),
             pl.BlockSpec((CHUNK, 4 * CHANNELS), lambda c: (c, 0)),
+            pl.BlockSpec((4 * WAVES // CHUNKS, CHANNELS), lambda c: (c, 0)),
         ],
         out_specs=(
             pl.BlockSpec((BAND * BAND, CHANNELS), const(0, 0)),
             pl.BlockSpec((NODES, CHUNK), lambda c: (0, c)),
+            pl.BlockSpec((4 * WAVES // CHUNKS, CHANNELS), lambda c: (c, 0)),
         ),
         scratch_shapes=[
-            pltpu.VMEM((FRAME * TILES, PICK), jnp.bfloat16),
-            pltpu.VMEM((FRAME * TILES, CHUNK), jnp.float32),
+            pltpu.VMEM((FRAME_ROWS, 4 * CHANNELS), jnp.bfloat16),
+            pltpu.VMEM((CHUNK // 128, FRAME_ROWS, 128), jnp.float32),
             pltpu.VMEM((NODES, 4 * CHANNELS), jnp.float32),
         ],
         compiler_params=pltpu.CompilerParams(vmem_limit_bytes=56 * MB),
         cost_estimate=pl.CostEstimate(
-            flops=2 * FRAME * TILES * RES * PICK,
+            flops=2 * (FRAME_ROWS + NODES) * RES * 4 * CHANNELS,
             bytes_accessed=24 * MB,
             transcendentals=NODES * RES,
         ),
@@ -686,14 +759,16 @@
         framed,
         halo,
         recur,
-        jnp.stack([row_at // 2, key]),
-        jnp.stack([input_gain, bias]),
+        input_index[None, :],
+        input_gain[None, :],
+        bias[None, :],
         readout,
+        spectral.reshape(4 * WAVES, CHANNELS),
     )
     return (
         blended.reshape(BAND, BAND, CHANNELS),
         upcoming.reshape(TILES, TILES, RES),
-        spectral,
+        spectral.reshape(2, 2, WAVES, CHANNELS),
     )
 
 

time: 86.2 us -> 75.7 us (0.88)
  local copies, waits for them, and re-layouts: 4 us -> 0 us
  other arithmetic: 3.55 us -> 0 us
  Pallas kernels: 77.5 us -> 74.7 us
    unnamed x4 -> x0, local copies, waits for them, and re-layouts: 2.16 us -> none
    another operation x2 -> x0, other arithmetic: 2 us -> none  [the longest x1 1.37 us: shards(): jnp.stack([input_gain, bias])]
    pallas_call x1, Pallas kernels: 16.6 us -> 14.7 us  [shards(): pl.pallas_call(reservoir_kernel, grid=(CHUNKS,), out_shape=(jax.ShapeDtyp...]
    add x2 -> x0, local copies, waits for them, and re-layouts: 1.53 us -> none  [shards(): slot_part = (2 * order + jnp.arange(2, dtype=jnp.int32)).reshape(-1)]
    pallas_call x1, Pallas kernels: 60.9 us -> 60 us  [shards(): pl.pallas_call(chain_kernel, out_shape=(jax.ShapeDtypeStruct((2, 2, WAVES...]
where the time goes in v2:
time: 75.7 us; the launch traced here: 75.4 us
  Pallas kernels  74.7 us (99%)
    pallas_call x1, Pallas kernels, shards(): pl.pallas_call(chain_kernel, out_shape=(jax.ShapeDtypeStruct((2, 2, WAVES...  60 us
    pallas_call x1, Pallas kernels, shards(): pl.pallas_call(reservoir_kernel, grid=(CHUNKS,), out_shape=(jax.ShapeDtyp...  14.7 us

profile of v2, /device:TPU:1, one launch (start us, length us, event | category | flops | bytes accessed | tf_op | source)
XLA Modules:
  0.0 75.4 jit_solution(8393793266413128504)
XLA Ops:
  0.6 60.0 %chain.1 = (f32[2,2,256,128]{3,2,1,0:T(8,128)}, bf16[16,56,384]{2,1,0:T(8,128)(2,1)}, bf16[2,56,256]{2,1,0:T(8,128)(2,1)}, f32[576,4096]{1,0:T(8,128)}) custom-call(s32[256]{0:T(256)} %slots_ref.1, s32[8,32]{1,0:T(8,128)} %bitcast.17, f32[2304,128]{1,0:T(8,128)} %bitcast.13, s32[1,256]{1,0:T(1,128)} %bitcast.18, ...), custom_call_target="tpu_custom_call" | custom-call | flops 4831838208 | bytes 31457280 | tf_op jit(solution)/shard_map/chain/pallas_call | solution.py:649
  60.6 14.7 %reservoir.1 = (f32[2304,128]{1,0:T(8,128)}, bf16[576,4096]{1,0:T(8,128)(2,1)}, f32[1024,128]{1,0:T(8,128)}) custom-call(bf16[16,56,384]{2,1,0:T(8,128)(2,1)} %get-tuple-element.10.rows_ref, bf16[2,56,256]{2,1,0:T(8,128)(2,1)} %get-tuple-element.11.halo_ref, f32[576,4096]{1,0:T(8,128)} %get-tuple-element.12.recur_ref, s32[1,4096]{1,0:T(1,128)} %bitcast.14, ...), custom_call_target="tpu_custom_call" | custom-call | flops 5502926848 | bytes 25165824 | tf_op jit(solution)/shard_map/reservoir/pallas_call | solution.py:723

commit v3 on v2

--- a/solution.py
+++ b/solution.py
@@ -28,11 +28,12 @@
 SENT_COLS = 2 * HALF
 TILES = 24
 FRAME = TILES + 2
-CHUNK = 512
+CHUNK = 1024
 CHUNKS = RES // CHUNK
 FRAME_ROWS = 736
 MB = 1 << 20
 MESH = pl.DeviceIdType.MESH
+FAR = (2, 1, 1, 0)
 SPLIT = (7, 16, 24, 32)
 LANES = SUB_ROWS * CHANNELS
 NODES = TILES * TILES
@@ -137,35 +138,32 @@
     chip = a * (LONS // 2) + lax.div(o, 2)
     sibling = (a, o + 1 - 2 * core)
 
-    def along(digit):
-        half = lax.div(digit, 2)
-        return (1 - half) * (2 - digit) + half * 3 * (3 - digit)
-
-    def moved(at, size, by):
-        return lax.rem(at + by, size)
+    z_lo, x = lax.div(a, 4), lax.rem(a, 4)
+    z_hi, y = lax.div(o, 8), lax.rem(lax.div(o, 2), 4)
+    along = (2, 1, 3, 0)
+    xs = [lax.rem(x + by, 4) for by in along]
+    ys = [lax.rem(y + by, 4) * 2 for by in along]
+    lats = [z * 4 + at for at in xs for z in (1 - z_lo, z_lo)]
+    sectors = [z * 8 + at for z in (1 - z_hi, z_hi) for at in ys]
+    partners = [(i, j) for i in range(LATS) for j in range(LONS // 2)]
+    hops = lambda ij: FAR[ij[0] // 2] + FAR[ij[1] % 4] + (1, 0)[ij[0] % 2] + (2, 0)[ij[1] // 4]
+    partners = sorted(partners[:-1], key=hops, reverse=True)
 
     def lon_at(step):
-        z = moved(lax.div(o, 8), 2, 1 - lax.div(step, 8))
-        y = moved(lax.rem(lax.div(o, 2), 4), 4, along(lax.rem(lax.div(step, 2), 4)))
-        return z * 8 + y * 2 + moved(core, 2, 1 - lax.rem(step, 2))
+        at = sectors[step // 2]
+        return at + (core if step % 2 else 1 - core)
 
     def chip_at(step):
-        z_hi = moved(lax.div(o, 8), 2, 1 - lax.div(step, 32))
-        x = moved(lax.rem(a, 4), 4, along(lax.rem(lax.div(step, 8), 4)))
-        y = moved(lax.rem(lax.div(o, 2), 4), 4, along(lax.rem(lax.div(step, 2), 4)))
-        z_lo = moved(lax.div(a, 4), 2, 1 - lax.rem(step, 2))
-        return (z_lo * 4 + x) * 8 + z_hi * 4 + y
+        i, j = partners[step]
+        return lats[i] * (LONS // 2) + lax.div(sectors[j], 2)
 
     def chip_device(step):
-        other = chip_at(step)
-        return (lax.div(other, LONS // 2), 2 * lax.rem(other, LONS // 2) + core)
+        i, j = partners[step]
+        return (lats[i], sectors[j] + core)
 
     def each(count, action):
-        def step(s, carry):
+        for s in range(count - 1):
             action(s)
-            return carry
-
-        lax.fori_loop(0, count - 1, step, 0)
 
     def load_states(b):
         return pltpu.make_async_copy(
@@ -291,7 +289,7 @@
             right = jnp.concatenate([blocks_ref[g, l] for l in range(CONN)], axis=1)
             recur_ref[:, pl.ds(pl.multiple_of(g * BLOCK, BLOCK), BLOCK)] = lax.dot_general(
                 left, right, (((1,), (1,)), ((), ())), preferred_element_type=jnp.float32
-            )
+            ).astype(jnp.bfloat16)
             return carry
 
         lax.fori_loop(first, last, one, 0)
@@ -339,12 +337,20 @@
         return pltpu.make_async_remote_copy(
             src_ref=message_ref.at[chip_at(s)],
             dst_ref=owned_ref.at[chip],
-            send_sem=out_send.at[s],
-            recv_sem=out_recv.at[s],
+            send_sem=out_send,
+            recv_sem=out_recv,
             device_id=chip_device(s),
             device_id_type=MESH,
         )
 
+    out_all = pltpu.make_async_remote_copy(
+        src_ref=message_ref.at[pl.ds(0, CHIPS - 1)],
+        dst_ref=owned_ref.at[pl.ds(0, CHIPS - 1)],
+        send_sem=out_send,
+        recv_sem=out_recv,
+        device_id=sibling,
+        device_id_type=MESH,
+    )
     each(CHIPS, lambda s: out_copy(s).start())
     owned_ref[chip] = message_ref[chip]
 
@@ -355,7 +361,7 @@
             preferred_element_type=jnp.float32,
         ).astype(jnp.bfloat16)
     stores.append(recur_blocks(1, SPLIT[0], SPLIT[1]))
-    each(CHIPS, lambda s: out_copy(s).wait_recv())
+    out_all.wait_recv()
 
     for r in range(SUB_ROWS):
         wide_ref[r] = (
@@ -409,16 +415,24 @@
         return pltpu.make_async_remote_copy(
             src_ref=reply_ref.at[chip_at(s)],
             dst_ref=replied_ref.at[chip],
-            send_sem=back_send.at[s],
-            recv_sem=back_recv.at[s],
+            send_sem=back_send,
+            recv_sem=back_recv,
             device_id=chip_device(s),
             device_id_type=MESH,
         )
 
+    back_all = pltpu.make_async_remote_copy(
+        src_ref=reply_ref.at[pl.ds(0, CHIPS - 1)],
+        dst_ref=replied_ref.at[pl.ds(0, CHIPS - 1)],
+        send_sem=back_send,
+        recv_sem=back_recv,
+        device_id=sibling,
+        device_id_type=MESH,
+    )
     each(CHIPS, lambda s: back_copy(s).start())
     replied_ref[chip] = reply_ref[chip]
     stores.append(recur_blocks(2, SPLIT[1], SPLIT[2]))
-    each(CHIPS, lambda s: back_copy(s).wait_recv())
+    back_all.wait_recv()
 
     whole = replied_ref[...].astype(jnp.float32)
     lower = whole[:, 0:4].reshape(2 * CHIPS * 2, LANES)
@@ -505,8 +519,8 @@
 
     lax.fori_loop(1, LONS - 1, arrived, 0)
     each(LONS, lambda s: row_copy(s).wait_send())
-    each(CHIPS, lambda s: out_copy(s).wait_send())
-    each(CHIPS, lambda s: back_copy(s).wait_send())
+    out_all.wait_send()
+    back_all.wait_send()
     each(LONS, lambda s: grid_copy(s).wait_send())
     to_sibling.wait_send()
     for_sibling.wait_send()
@@ -600,13 +614,14 @@
         kept = [shifted(0), shifted(1)]
         for i in range(0, TILES, 2):
             both = []
+            recur = recur_ref[i * TILES : (i + 2) * TILES, lanes].astype(jnp.float32)
             for step in range(2):
                 kept.append(shifted(i + step + 2))
                 near, next_one, far = kept
                 picked = jnp.where(row_two, far, jnp.where(row_one, next_one, near))
                 kept = kept[1:]
-                at = (i + step) * TILES
-                both.append(jnp.tanh(recur_ref[at : at + TILES, lanes] + picked * gain + bias))
+                part = recur[step * TILES : (step + 1) * TILES]
+                both.append(jnp.tanh(part + picked * gain + bias))
             next_ref[i * TILES : (i + 2) * TILES, lanes] = jnp.concatenate(both, axis=0).astype(
                 jnp.bfloat16
             )
@@ -652,14 +667,14 @@
             jax.ShapeDtypeStruct((2, 2, WAVES, CHANNELS), jnp.float32),
             jax.ShapeDtypeStruct((LONS, SENT_COLS, LANES), jnp.bfloat16),
             jax.ShapeDtypeStruct((2, SENT_COLS, 2 * CHANNELS), jnp.bfloat16),
-            jax.ShapeDtypeStruct((NODES, RES), jnp.float32),
+            jax.ShapeDtypeStruct((NODES, RES), jnp.bfloat16),
         ),
         in_specs=[smem] * 2 + [vmem] * 10 + [hbm] * 2,
         out_specs=(vmem, vmem, vmem, hbm),
         scratch_shapes=[
             bf16((RES // BLOCK, NODES, BLOCK)),
             bf16((RES // BLOCK, CONN, BLOCK, BLOCK)),
-            f32((NODES, RES)),
+            bf16((NODES, RES)),
             bf16((LONS, SUB_ROWS * BAND, CHANNELS)),
             bf16((LONS, SUB_ROWS * BAND, CHANNELS)),
             bf16((2 * WAVES, 2 * WAVES)),
@@ -686,10 +701,10 @@
             pltpu.SemaphoreType.DMA((LONS,)),
             pltpu.SemaphoreType.DMA((2,)),
             pltpu.SemaphoreType.DMA((2,)),
-            pltpu.SemaphoreType.DMA((CHIPS,)),
-            pltpu.SemaphoreType.DMA((CHIPS,)),
-            pltpu.SemaphoreType.DMA((CHIPS,)),
-            pltpu.SemaphoreType.DMA((CHIPS,)),
+            pltpu.SemaphoreType.DMA,
+            pltpu.SemaphoreType.DMA,
+            pltpu.SemaphoreType.DMA,
+            pltpu.SemaphoreType.DMA,
             pltpu.SemaphoreType.DMA((LONS,)),
             pltpu.SemaphoreType.DMA((LONS,)),
             pltpu.SemaphoreType.DMA((2,)),

time: 75.7 us -> 67.2 us (0.89)
  Pallas kernels: 74.7 us -> 65.7 us
    pallas_call x1, Pallas kernels: 60 us -> 54 us  [shards(): pl.pallas_call(chain_kernel, out_shape=(jax.ShapeDtypeStruct((2, 2, WAVES...]
    pallas_call x1, Pallas kernels: 14.7 us -> 11.7 us  [shards(): pl.pallas_call(reservoir_kernel, grid=(CHUNKS,), out_shape=(jax.ShapeDtyp...]
where the time goes in v3:
time: 67.2 us; the launch traced here: 66.3 us
  Pallas kernels  65.7 us (98%)
    pallas_call x1, Pallas kernels, shards(): pl.pallas_call(chain_kernel, out_shape=(jax.ShapeDtypeStruct((2, 2, WAVES...  54 us
    pallas_call x1, Pallas kernels, shards(): pl.pallas_call(reservoir_kernel, grid=(CHUNKS,), out_shape=(jax.ShapeDtyp...  11.7 us

profile of v3, /device:TPU:1, one launch (start us, length us, event | category | flops | bytes accessed | tf_op | source)
XLA Modules:
  0.0 66.3 jit_solution(6247371186205531891)
XLA Ops:
  0.6 54.0 %chain.1 = (f32[2,2,256,128]{3,2,1,0:T(8,128)}, bf16[16,56,384]{2,1,0:T(8,128)(2,1)}, bf16[2,56,256]{2,1,0:T(8,128)(2,1)}, bf16[576,4096]{1,0:T(8,128)(2,1)}) custom-call(s32[256]{0:T(256)} %slots_ref.1, s32[8,32]{1,0:T(8,128)} %bitcast.17, f32[2304,128]{1,0:T(8,128)} %bitcast.13, s32[1,256]{1,0:T(1,128)} %bitcast.18, ...), custom_call_target="tpu_custom_call" | custom-call | flops 4831838208 | bytes 31457280 | tf_op jit(solution)/shard_map/chain/pallas_call | solution.py:664
  54.6 11.7 %reservoir.1 = (f32[2304,128]{1,0:T(8,128)}, bf16[576,4096]{1,0:T(8,128)(2,1)}, f32[1024,128]{1,0:T(8,128)}) custom-call(bf16[16,56,384]{2,1,0:T(8,128)(2,1)} %get-tuple-element.10.rows_ref, bf16[2,56,256]{2,1,0:T(8,128)(2,1)} %get-tuple-element.11.halo_ref, bf16[576,4096]{1,0:T(8,128)(2,1)} %get-tuple-element.12.recur_ref, s32[1,4096]{1,0:T(1,128)} %bitcast.14, ...), custom_call_target="tpu_custom_call" | custom-call | flops 5502926848 | bytes 25165824 | tf_op jit(solution)/shard_map/reservoir/pallas_call | solution.py:738

commit v4 on v3

--- a/solution.py
+++ b/solution.py
@@ -34,7 +34,7 @@
 MB = 1 << 20
 MESH = pl.DeviceIdType.MESH
 FAR = (2, 1, 1, 0)
-SPLIT = (7, 16, 24, 32)
+SPLIT = (5, 18, 31, 32)
 LANES = SUB_ROWS * CHANNELS
 NODES = TILES * TILES
 
@@ -78,22 +78,27 @@
 def chain_kernel(
     slots_ref,
     index_ref,
-    fields_ref,
     order_ref,
-    forward_high_ref,
-    forward_low_ref,
-    inverse_ref,
     cos_ref,
     log_sin_ref,
     weight_ref,
     diffusion_ref,
     logs_ref,
+    fields_hbm,
+    forward_high_hbm,
+    forward_low_hbm,
+    inverse_hbm,
     states_hbm,
     blocks_hbm,
-    spectral_ref,
+    spectral_hbm,
     framed_ref,
     halo_ref,
     recur_hbm,
+    fields_ref,
+    forward_high_ref,
+    forward_low_ref,
+    inverse_ref,
+    spectral_ref,
     states_ref,
     blocks_ref,
     recur_ref,
@@ -116,7 +121,9 @@
     mine_ref,
     other_ref,
     inverted_ref,
+    partial_ref,
     samples_ref,
+    early_sem,
     load_sem,
     store_sem,
     lon_send,
@@ -174,6 +181,20 @@
 
     load_blocks = pltpu.make_async_copy(blocks_hbm, blocks_ref, load_sem.at[RES // BLOCK])
 
+    load_fields = pltpu.make_async_copy(fields_hbm, fields_ref, early_sem.at[0])
+    load_tables = [
+        pltpu.make_async_copy(source, target, early_sem.at[at + 1])
+        for at, (source, target) in enumerate(
+            (
+                (forward_high_hbm, forward_high_ref),
+                (forward_low_hbm, forward_low_ref),
+                (inverse_hbm, inverse_ref),
+            )
+        )
+    ]
+    store_spectral = pltpu.make_async_copy(spectral_ref, spectral_hbm, early_sem.at[4])
+    load_fields.start()
+
     barrier = pltpu.get_barrier_semaphore()
     each(
         CHIPS,
@@ -181,18 +202,19 @@
             barrier, inc=1, device_id=chip_device(s), device_id_type=MESH
         ),
     )
-    each(
-        LONS,
-        lambda s: pl.semaphore_signal(
-            barrier, inc=1, device_id=(a, lon_at(s)), device_id_type=MESH
-        ),
-    )
+    for step in range(0, LONS, 2):
+        pl.semaphore_signal(
+            barrier, inc=1, device_id=(a, lon_at(step)), device_id_type=MESH
+        )
+    for load in load_tables:
+        load.start()
     load_blocks.start()
     each(RES // BLOCK + 1, lambda b: load_states(b).start())
     halo_ref[...] = jnp.zeros_like(halo_ref)
+    load_fields.wait()
     for d in range(LONS):
         sent_ref[d] = fields_ref[d * 144 : (d + 1) * 144, :].astype(jnp.bfloat16)
-    pl.semaphore_wait(barrier, LONS + CHIPS - 2)
+    pl.semaphore_wait(barrier, CHIPS - 1 + LONS // 2)
 
     def row_copy(s):
         return pltpu.make_async_remote_copy(
@@ -207,6 +229,8 @@
     each(LONS, lambda s: row_copy(s).start())
     rows_ref[o] = sent_ref[o]
 
+    for load in load_tables:
+        load.wait()
     column = lax.broadcasted_iota(jnp.int32, (WAVES, 2 * WAVES), 1)
     slot = 4 * ((column >> 2) & (CHIPS - 1)) + 2 * (column >> 8) + ((column >> 1) & 1)
     moves = jnp.where(lax.broadcasted_iota(jnp.int32, slot.shape, 0) == slot, 1.0, 0.0)
@@ -274,7 +298,10 @@
     lax.fori_loop(0, WAVES // 8, eight, ((zero, zero), (zero, zero)))
     for s in range(2):
         table = legendre_ref[s]
-        plain_ref[s] = table.astype(jnp.bfloat16)
+        turned = table.T
+        high = turned.astype(jnp.bfloat16)
+        low = (turned - high.astype(jnp.float32)).astype(jnp.bfloat16)
+        plain_ref[s] = jnp.concatenate([high, low, high], axis=1)
         table = table * weight_ref[...]
         high = table.astype(jnp.bfloat16)
         weighted_ref[0, s] = high
@@ -393,10 +420,11 @@
         )
         for p in range(2):
             spectral_ref[s, p] = filtered[:, p * 128 : (p + 1) * 128]
-        grid = lax.dot_general(
+        high = filtered.astype(jnp.bfloat16)
+        low = (filtered - high.astype(jnp.float32)).astype(jnp.bfloat16)
+        grid = jnp.dot(
             plain_ref[s],
-            filtered.astype(jnp.bfloat16),
-            (((0,), (0,)), ((), ())),
+            jnp.concatenate([high, high, low], axis=0),
             preferred_element_type=jnp.float32,
         )
         for p in range(2):
@@ -430,6 +458,7 @@
         device_id_type=MESH,
     )
     each(CHIPS, lambda s: back_copy(s).start())
+    store_spectral.start()
     replied_ref[chip] = reply_ref[chip]
     stores.append(recur_blocks(2, SPLIT[1], SPLIT[2]))
     back_all.wait_recv()
@@ -448,37 +477,44 @@
     )
     for_sibling.start()
     kept = jnp.where(core == 0, lower, upper).astype(jnp.bfloat16)
-    own = jnp.dot(inverted_ref[core], kept, preferred_element_type=jnp.float32)
+    partial = jnp.dot(inverted_ref[core], kept, preferred_element_type=jnp.float32)
+    for r in range(SUB_ROWS):
+        partial_ref[r] = partial[:, r * 128 : (r + 1) * 128]
     for_sibling.wait_recv()
-    own += jnp.dot(inverted_ref[1 - core], mine_ref[...], preferred_element_type=jnp.float32)
-    for d in range(LONS):
-        samples_ref[d] = own[d * SENT_COLS : (d + 1) * SENT_COLS].astype(jnp.bfloat16)
-
-    def grid_copy(s):
+
+    def grid_copy(r, s):
         return pltpu.make_async_remote_copy(
-            src_ref=samples_ref.at[lon_at(s)],
-            dst_ref=framed_ref.at[o],
-            send_sem=grid_send.at[s],
-            recv_sem=grid_recv.at[o],
+            src_ref=samples_ref.at[r, lon_at(s)],
+            dst_ref=framed_ref.at[r, o],
+            send_sem=grid_send,
+            recv_sem=grid_recv.at[r, o],
             device_id=(a, lon_at(s)),
             device_id_type=MESH,
         )
 
-    def grid_from(source):
+    def grid_from(r, source):
         return pltpu.make_async_remote_copy(
-            src_ref=samples_ref.at[source],
-            dst_ref=framed_ref.at[source],
-            send_sem=grid_send.at[LONS - 1],
-            recv_sem=grid_recv.at[source],
-            device_id=(a, source),
+            src_ref=samples_ref.at[r, source],
+            dst_ref=framed_ref.at[r, source],
+            send_sem=grid_send,
+            recv_sem=grid_recv.at[r, source],
+            device_id=sibling,
             device_id_type=MESH,
         )
 
-    each(LONS, lambda s: grid_copy(s).start())
-    framed_ref[o] = samples_ref[o]
+    edge = lax.div(o, LONS // 2)
+    for r in (1, 2 * edge, 2 - 2 * edge):
+        lanes = pl.ds(pl.multiple_of(r * CHANNELS, CHANNELS), CHANNELS)
+        sample = partial_ref[r] + jnp.dot(
+            inverted_ref[1 - core], mine_ref[:, lanes], preferred_element_type=jnp.float32
+        )
+        samples_ref[r] = sample.reshape(LONS, SENT_COLS, CHANNELS).astype(jnp.bfloat16)
+        each(LONS, lambda s: grid_copy(r, s).start())
+        framed_ref[r, o] = samples_ref[r, o]
     stores.append(recur_blocks(3, SPLIT[2], SPLIT[3]))
+
     up = pltpu.make_async_remote_copy(
-        src_ref=framed_ref.at[LONS - 1, :, pl.ds(CHANNELS, 2 * CHANNELS)],
+        src_ref=framed_ref.at[pl.ds(1, 2), LONS - 1],
         dst_ref=halo_ref.at[0],
         send_sem=halo_send.at[0],
         recv_sem=halo_recv.at[0],
@@ -486,7 +522,7 @@
         device_id_type=MESH,
     )
     down = pltpu.make_async_remote_copy(
-        src_ref=framed_ref.at[0, :, pl.ds(0, 2 * CHANNELS)],
+        src_ref=framed_ref.at[pl.ds(0, 2), 0],
         dst_ref=halo_ref.at[1],
         send_sem=halo_send.at[1],
         recv_sem=halo_recv.at[1],
@@ -496,7 +532,8 @@
 
     @pl.when(o < LONS - 1)
     def _():
-        grid_from(LONS - 1).wait_recv()
+        grid_from(1, LONS - 1).wait_recv()
+        grid_from(2, LONS - 1).wait_recv()
 
     @pl.when(a < LATS - 1)
     def _():
@@ -504,26 +541,45 @@
 
     @pl.when(o > 0)
     def _():
-        grid_from(0).wait_recv()
+        grid_from(1, 0).wait_recv()
+        grid_from(0, 0).wait_recv()
 
     @pl.when(a > 0)
     def _():
         down.start()
+
+    @pl.when(o < LONS - 1)
+    def _():
+        grid_from(0, LONS - 1).wait_recv()
+
+    @pl.when(o > 0)
+    def _():
+        grid_from(2, 0).wait_recv()
 
     def arrived(source, carry):
         @pl.when(source != o)
         def _():
-            grid_from(source).wait_recv()
+            for r in range(SUB_ROWS):
+                grid_from(r, source).wait_recv()
 
         return carry
 
     lax.fori_loop(1, LONS - 1, arrived, 0)
+    grid_all = pltpu.make_async_remote_copy(
+        src_ref=samples_ref.at[:, pl.ds(0, LONS - 1)],
+        dst_ref=framed_ref.at[:, pl.ds(0, LONS - 1)],
+        send_sem=grid_send,
+        recv_sem=grid_recv.at[0, 0],
+        device_id=sibling,
+        device_id_type=MESH,
+    )
     each(LONS, lambda s: row_copy(s).wait_send())
     out_all.wait_send()
     back_all.wait_send()
-    each(LONS, lambda s: grid_copy(s).wait_send())
+    grid_all.wait_send()
     to_sibling.wait_send()
     for_sibling.wait_send()
+    store_spectral.wait()
     for copy in stores:
         copy.wait()
 
@@ -561,14 +617,11 @@
     def _():
         def row_of(position):
             if position < 2:
-                part = halo_ref[0, :, position * 128 : (position + 1) * 128]
+                part = halo_ref[0, position]
             elif position >= BAND + 2:
-                at = position - BAND - 2
-                part = halo_ref[1, :, at * 128 : (at + 1) * 128]
+                part = halo_ref[1, position - BAND - 2]
             else:
-                j = position - 2
-                at = j % SUB_ROWS
-                part = rows_ref[j // SUB_ROWS, :, at * 128 : (at + 1) * 128]
+                part = rows_ref[(position - 2) % SUB_ROWS, (position - 2) // SUB_ROWS]
             return part.astype(jnp.float32)
 
         for group in range(0, FRAME, 4):
@@ -665,13 +718,18 @@
         chain_kernel,
         out_shape=(
             jax.ShapeDtypeStruct((2, 2, WAVES, CHANNELS), jnp.float32),
-            jax.ShapeDtypeStruct((LONS, SENT_COLS, LANES), jnp.bfloat16),
-            jax.ShapeDtypeStruct((2, SENT_COLS, 2 * CHANNELS), jnp.bfloat16),
+            jax.ShapeDtypeStruct((SUB_ROWS, LONS, SENT_COLS, CHANNELS), jnp.bfloat16),
+            jax.ShapeDtypeStruct((2, 2, SENT_COLS, CHANNELS), jnp.bfloat16),
             jax.ShapeDtypeStruct((NODES, RES), jnp.bfloat16),
         ),
-        in_specs=[smem] * 2 + [vmem] * 10 + [hbm] * 2,
-        out_specs=(vmem, vmem, vmem, hbm),
+        in_specs=[smem] * 2 + [vmem] * 6 + [hbm] * 6,
+        out_specs=(hbm, vmem, vmem, hbm),
         scratch_shapes=[
+            f32((BAND * BAND, CHANNELS)),
+            bf16((2 * WAVES, COLS)),
+            bf16((2 * WAVES, COLS)),
+            bf16((LONS * SENT_COLS, 2 * WAVES)),
+            f32((2, 2, WAVES, CHANNELS)),
             bf16((RES // BLOCK, NODES, BLOCK)),
             bf16((RES // BLOCK, CONN, BLOCK, BLOCK)),
             bf16((NODES, RES)),
@@ -682,7 +740,7 @@
             f32((2, 3, WAVES, CHANNELS)),
             f32((2, WAVES, ROWS)),
             bf16((2, 2, WAVES, ROWS)),
-            bf16((2, WAVES, ROWS)),
+            bf16((2, ROWS, 3 * WAVES)),
             bf16((WAVES, LANES)),
             bf16((WAVES, LANES)),
             bf16((CHIPS, 8, LANES)),
@@ -694,7 +752,9 @@
             bf16((WAVES, LANES)),
             bf16((WAVES, LANES)),
             bf16((2, LONS * SENT_COLS, WAVES)),
-            bf16((LONS, SENT_COLS, LANES)),
+            f32((SUB_ROWS, LONS * SENT_COLS, CHANNELS)),
+            bf16((SUB_ROWS, LONS, SENT_COLS, CHANNELS)),
+            pltpu.SemaphoreType.DMA((5,)),
             pltpu.SemaphoreType.DMA((RES // BLOCK + 1,)),
             pltpu.SemaphoreType.DMA((4,)),
             pltpu.SemaphoreType.DMA((LONS,)),
@@ -705,8 +765,8 @@
             pltpu.SemaphoreType.DMA,
             pltpu.SemaphoreType.DMA,
             pltpu.SemaphoreType.DMA,
-            pltpu.SemaphoreType.DMA((LONS,)),
-            pltpu.SemaphoreType.DMA((LONS,)),
+            pltpu.SemaphoreType.DMA,
+            pltpu.SemaphoreType.DMA((SUB_ROWS, LONS)),
             pltpu.SemaphoreType.DMA((2,)),
             pltpu.SemaphoreType.DMA((2,)),
         ],
@@ -720,16 +780,16 @@
     )(
         wave_slots,
         adjacency_index.T,
-        fields.reshape(BAND * BAND, CHANNELS),
         wave_slots[None, :],
-        jnp.asarray(forward_high),
-        jnp.asarray(forward_low),
-        jnp.asarray(inverse_columns(), jnp.bfloat16),
         jnp.asarray(cos_col[None, :], jnp.float32),
         jnp.asarray(np.log(sin_col)[None, :], jnp.float32),
         jnp.asarray((math.pi / ROWS) * sin_col[None, :], jnp.float32),
         diffusion[None, :],
         jnp.asarray(log_terms()[None, :], jnp.float32),
+        fields.reshape(BAND * BAND, CHANNELS),
+        jnp.asarray(forward_high),
+        jnp.asarray(forward_low),
+        jnp.asarray(inverse_columns(), jnp.bfloat16),
         reservoir_state.reshape(NODES, RES),
         adjacency_blocks,
     )
@@ -744,8 +804,8 @@
             jax.ShapeDtypeStruct((4 * WAVES, CHANNELS), jnp.float32),
         ),
         in_specs=[
-            pl.BlockSpec((LONS, SENT_COLS, LANES), const(0, 0, 0)),
-            pl.BlockSpec((2, SENT_COLS, 2 * CHANNELS), const(0, 0, 0)),
+            pl.BlockSpec((SUB_ROWS, LONS, SENT_COLS, CHANNELS), const(0, 0, 0, 0)),
+            pl.BlockSpec((2, 2, SENT_COLS, CHANNELS), const(0, 0, 0, 0)),
             pl.BlockSpec((NODES, CHUNK), lambda c: (0, c)),
             pl.BlockSpec((1, CHUNK), lambda c: (0, c)),
             pl.BlockSpec((1, CHUNK), lambda c: (0, c)),

time: 67.2 us -> 66.3 us (0.987)
  no operation moved by 1% of the time
where the time goes in v4:
time: 66.3 us; the launch traced here: 66 us
  Pallas kernels  65.4 us (99%)
    pallas_call x1, Pallas kernels, shards(): pl.pallas_call(chain_kernel, out_shape=(jax.ShapeDtypeStruct((2, 2, WAVES...  53.7 us
    pallas_call x1, Pallas kernels, shards(): pl.pallas_call(reservoir_kernel, grid=(CHUNKS,), out_shape=(jax.ShapeDtyp...  11.7 us

profile of v4, /device:TPU:1, one launch (start us, length us, event | category | flops | bytes accessed | tf_op | source)
XLA Modules:
  0.0 66.0 jit_solution(1782083023688256456)
XLA Ops:
  0.6 53.7 %chain.1 = (f32[2,2,256,128]{3,2,1,0:T(8,128)}, bf16[3,16,56,128]{3,2,1,0:T(8,128)(2,1)}, bf16[2,2,56,128]{3,2,1,0:T(8,128)(2,1)}, bf16[576,4096]{1,0:T(8,128)(2,1)}) custom-call(s32[256]{0:T(256)} %slots_ref.1, s32[8,32]{1,0:T(8,128)} %bitcast.17, s32[1,256]{1,0:T(1,128)} %bitcast.18, f32[1,384]{1,0:T(1,128)} %constant.14.clone.cos_ref, ...), custom_call_target="tpu_custom_call" | custom-call | flops 4831838208 | bytes 31457280 | tf_op jit(solution)/shard_map/chain/pallas_call | solution.py:717
  54.3 11.7 %reservoir.1 = (f32[2304,128]{1,0:T(8,128)}, bf16[576,4096]{1,0:T(8,128)(2,1)}, f32[1024,128]{1,0:T(8,128)}) custom-call(bf16[3,16,56,128]{3,2,1,0:T(8,128)(2,1)} %get-tuple-element.10.rows_ref, bf16[2,2,56,128]{3,2,1,0:T(8,128)(2,1)} %get-tuple-element.11.halo_ref, bf16[576,4096]{1,0:T(8,128)(2,1)} %get-tuple-element.12.recur_ref, s32[1,4096]{1,0:T(1,128)} %bitcast.14, ...), custom_call_target="tpu_custom_call" | custom-call | flops 5502926848 | bytes 25165824 | tf_op jit(solution)/shard_map/reservoir/pallas_call | solution.py:798

commit v5 on v4

--- a/solution.py
+++ b/solution.py
@@ -30,7 +30,7 @@
 FRAME = TILES + 2
 CHUNK = 1024
 CHUNKS = RES // CHUNK
-FRAME_ROWS = 736
+FRAME_ROWS = 688
 MB = 1 << 20
 MESH = pl.DeviceIdType.MESH
 FAR = (2, 1, 1, 0)
@@ -624,16 +624,16 @@
                 part = rows_ref[(position - 2) % SUB_ROWS, (position - 2) // SUB_ROWS]
             return part.astype(jnp.float32)
 
-        for group in range(0, FRAME, 4):
+        for group in range(0, FRAME, 8):
             for a in range(2):
-                parts = [row_of(2 * i + a) for i in range(group, min(group + 4, FRAME))]
+                parts = [row_of(2 * i + a) for i in range(group, min(group + 8, FRAME))]
                 for b in range(2):
-                    block = [part[b * HALF : (b + 1) * HALF] for part in parts]
-                    if len(block) < 4:
-                        block.append(jnp.zeros((FRAME_ROWS - FRAME * HALF, CHANNELS), jnp.float32))
+                    block = [part[b * HALF : b * HALF + FRAME] for part in parts]
+                    if len(block) < 8:
+                        block.append(jnp.zeros((FRAME_ROWS - FRAME * FRAME, CHANNELS), jnp.float32))
                     block = jnp.concatenate(block, axis=0)
                     at = (a * 2 + b) * 128
-                    frame_ref[group * HALF : group * HALF + block.shape[0], at : at + 128] = (
+                    frame_ref[group * FRAME : group * FRAME + block.shape[0], at : at + 128] = (
                         block.astype(jnp.bfloat16)
                     )
         total_ref[...] = jnp.zeros_like(total_ref)
@@ -660,7 +660,7 @@
 
         def shifted(i):
             near, next_one, far = [
-                drive_ref[q, i * HALF + k : i * HALF + k + TILES, :] for k in range(3)
+                drive_ref[q, i * FRAME + k : i * FRAME + k + TILES, :] for k in range(3)
             ]
             return jnp.where(col_two, far, jnp.where(col_one, next_one, near))
 
@@ -687,7 +687,7 @@
                 at = (a * 2 + b) * 128
                 forecast = frame_ref[:, at : at + 128].astype(jnp.float32)
                 for i in range(TILES):
-                    start = (i + 1) * HALF + 1
+                    start = (i + 1) * FRAME + 1
                     blend_ref[pl.ds((2 * i + a) * BAND + b, TILES, stride=2), :] = (
                         forecast[start : start + TILES]
                         + total_ref[i * TILES : (i + 1) * TILES, at : at + 128]

time: 66.3 us -> 66.1 us (level)
  no operation moved by 1% of the time
where the time goes in v5:
time: 66.1 us; the launch traced here: 65.8 us
  Pallas kernels  65.2 us (99%)
    pallas_call x1, Pallas kernels, shards(): pl.pallas_call(chain_kernel, out_shape=(jax.ShapeDtypeStruct((2, 2, WAVES...  53.7 us
    pallas_call x1, Pallas kernels, shards(): pl.pallas_call(reservoir_kernel, grid=(CHUNKS,), out_shape=(jax.ShapeDtyp...  11.5 us

profile of v5, /device:TPU:1, one launch (start us, length us, event | category | flops | bytes accessed | tf_op | source)
XLA Modules:
  0.0 65.8 jit_solution(3342223993002943918)
XLA Ops:
  0.6 53.7 %chain.1 = (f32[2,2,256,128]{3,2,1,0:T(8,128)}, bf16[3,16,56,128]{3,2,1,0:T(8,128)(2,1)}, bf16[2,2,56,128]{3,2,1,0:T(8,128)(2,1)}, bf16[576,4096]{1,0:T(8,128)(2,1)}) custom-call(s32[256]{0:T(256)} %slots_ref.1, s32[8,32]{1,0:T(8,128)} %bitcast.17, s32[1,256]{1,0:T(1,128)} %bitcast.18, f32[1,384]{1,0:T(1,128)} %constant.14.clone.cos_ref, ...), custom_call_target="tpu_custom_call" | custom-call | flops 4831838208 | bytes 31457280 | tf_op jit(solution)/shard_map/chain/pallas_call | solution.py:717
  54.3 11.5 %reservoir.1 = (f32[2304,128]{1,0:T(8,128)}, bf16[576,4096]{1,0:T(8,128)(2,1)}, f32[1024,128]{1,0:T(8,128)}) custom-call(bf16[3,16,56,128]{3,2,1,0:T(8,128)(2,1)} %get-tuple-element.10.rows_ref, bf16[2,2,56,128]{3,2,1,0:T(8,128)(2,1)} %get-tuple-element.11.halo_ref, bf16[576,4096]{1,0:T(8,128)(2,1)} %get-tuple-element.12.recur_ref, s32[1,4096]{1,0:T(1,128)} %bitcast.14, ...), custom_call_target="tpu_custom_call" | custom-call | flops 5301600256 | bytes 25165824 | tf_op jit(solution)/shard_map/reservoir/pallas_call | solution.py:798
